TPU v7x, 256 devices: a whole 4x4x8 slice. The times are simulated.
256 devices in a mesh: sector: 16 (over y_lo, x, core), sub: 16 (over z, y_hi).
Axes of the slice: x: 4, y: 4 (y_hi: 2, y_lo: 2; y = y_hi * 2 + y_lo), z: 8, core: 2. Of those that a mesh axis runs over, the one named last changes fastest.
Arguments:
- dual_load: float32 [16, 16, 2, 512, 256], P('sector', 'sub'), may hold values from -50 to 50
- flexibility: bfloat16 [16, 16, 2048, 2048], P('sector', 'sub'), may hold values from -10 to 10, as said below
- face_order: int32 [16, 16, 2048], P('sector', 'sub'), may hold values from 0 to 2047, each once within a row
- corner_index: int32 [16, 16, 32], P('sector', 'sub'), may hold values from 0 to 2047, as said below
- coarse_inverse: float32 [512, 512], replicated, may hold values from -10 to 10, as said below
Outputs:
- multiplier: float32 [16, 16, 2, 512, 256], P('sector', 'sub')
- residual: float32 [16, 16, 2, 512, 256], P('sector', 'sub')
Inputs may be any that keep to these rules, and one draw needn't show every extreme that they name: `flexibility`: a block of sizes of order one with a dominant diagonal; each subdomain's matrix is symmetric positive definite. `corner_index`: entries within one subdomain are distinct. `face_order`: each subdomain's row names every face slot once. `coarse_inverse`: symmetric positive definite with a dominant diagonal.
All inputs are finite; a program needn't handle non-finite values.
Results may differ from a plain program's by a relative error of at most 0.0087.
The roundings to bfloat16 on the way count: a program that leaves them out, or rounds other values in their place, can miss the bound.
Values may be sent and summed in bfloat16 or wider, within the bound.
A program may use at most 128 MiB of HBM per device.

v0:
```python
import jax
import jax.numpy as jnp
from jax import lax
from jax.sharding import PartitionSpec as P

ITERS = 2


def passed_along(x, axis, by):
    count = lax.axis_size(axis)
    pairs = [(i, i + by) for i in range(count) if 0 <= i + by < count]
    return lax.ppermute(x, axis, pairs)


def from_behind(value, axis, steps):
    count = lax.axis_size(axis)
    pairs = [(source, (source + steps) % count) for source in range(count)]
    return lax.ppermute(value, axis, pairs)


def squares(residual):
    return lax.psum(jnp.sum(residual * residual, axis=(0, 1, 2, 3)), ("sector", "sub"))


def inner_sum(left, right):
    return jnp.sum(left * right, axis=(0, 1, 2, 3))


def shards(dual_load, flexibility, face_order, corner_index, coarse_inverse):
    slot_order = face_order[0, 0]
    corners = corner_index[0, 0]
    corner_count = corners.shape[0]
    matrix = jnp.take(jnp.take(flexibility[0, 0], slot_order, axis=0), slot_order, axis=1)
    face_width = slot_order.shape[0] // 4
    cases = dual_load.shape[-1]
    sub_count = lax.axis_size("sub")
    multiplier = jnp.zeros_like(dual_load)
    residual = dual_load
    direction = dual_load
    norm_now = squares(residual)
    for iteration in range(ITERS):
        rounded = direction[0, 0].astype(jnp.bfloat16)
        lower_sub = passed_along(rounded[0], "sub", 1)
        previous = from_behind(rounded[1], "sector", 1)
        face_stack = jnp.concatenate([-lower_sub, rounded[0], -previous, rounded[1]], axis=0)
        partial_value = jnp.take(face_stack, corners, axis=0).astype(jnp.float32)
        sector_total = lax.psum(partial_value.astype(jnp.bfloat16), "sub").astype(jnp.float32)
        sector_id = lax.axis_index("sector")
        everything = lax.all_gather(sector_total, "sector", axis=0, tiled=True)
        inverse_rows = lax.dynamic_slice_in_dim(
            coarse_inverse, sector_id * corner_count, corner_count, 0
        )
        coarse = jnp.dot(
            inverse_rows,
            everything,
            precision=lax.Precision.HIGHEST,
            preferred_element_type=jnp.float32,
        )
        coarse = coarse / sub_count
        correction = jnp.zeros((4 * face_width, cases), jnp.float32).at[corners].add(coarse)
        product = jnp.dot(matrix, face_stack, preferred_element_type=jnp.float32) + correction
        outgoing_sub = product[:face_width]
        outgoing_cycle = product[2 * face_width : 3 * face_width]
        upper_next = passed_along(outgoing_sub.astype(jnp.bfloat16), "sub", -1)
        cycle_next = from_behind(outgoing_cycle.astype(jnp.bfloat16), "sector", -1)
        own_sub = product[face_width : 2 * face_width]
        own_cycle = product[3 * face_width :]
        jump_pair = jnp.stack(
            [own_sub - upper_next.astype(jnp.float32), own_cycle - cycle_next.astype(jnp.float32)],
            axis=0,
        )
        image = jump_pair[None, None]
        curvature = lax.psum(inner_sum(direction, image), ("sector", "sub"))
        alpha = norm_now / curvature
        multiplier = multiplier + alpha * direction
        residual = residual - alpha * image
        if iteration + 1 < ITERS:
            norm_next = squares(residual)
            direction = residual + norm_next / norm_now * direction
            norm_now = norm_next
    return (multiplier, residual)


def solution(mesh):
    return jax.shard_map(
        shards,
        mesh=mesh,
        in_specs=(
            P("sector", "sub", None, None, None),
            P("sector", "sub", None, None),
            P("sector", "sub", None),
            P("sector", "sub", None),
            P(),
        ),
        out_specs=(P("sector", "sub", None, None, None), P("sector", "sub", None, None, None)),
        check_vma=False,
    )
```

profile of v0, /device:TPU:1, one launch (start us, length us, event | category | flops | bytes accessed | tf_op | source)
XLA Modules:
  0.0 558.0 jit_solution(7757382936450684341)
XLA Ops:
  0.6 0.0 copy-start
  0.6 0.0 copy-start.5
  0.7 0.0 copy-start.4
  0.7 1.4 convert_element_type.34
  2.1 2.7 collective-permute-start.1
  4.8 4.8 collective-permute-start
  9.6 0.0 copy-done.5
  9.6 0.0 copy-done.4
  9.7 20.8 %gather_fusion = bf16[2048,2048]{1,0:T(8,128)(2,1)} fusion(bf16[2048,2048]{1,0:T(8,128)(2,1)} %bitcast.51, s32[2048]{0:T(1024)S(1)} %broadcast_clamp_fusion), kind=kCustom, calls=%fused_computation.2 | custom fusion | bytes 16785408 | tf_op jit(solution)/shard_map/jit(_take)/gather | solution.py:33
  30.5 7.4 %broadcast_select_fusion = bf16[2048,2048]{1,0:T(8,128)(2,1)} fusion(bf16[2048,2048]{1,0:T(8,128)(2,1)} %gather_fusion, pred[2048]{0:T(1024)(128)(4,1)S(1)} %compare_and_fusion), kind=kLoop, calls=%fused_computation.6 | loop fusion | flops 4194304 | bytes 16779264 | tf_op jit(solution)/shard_map/jit(_take)/select_n | solution.py:33
  37.9 12.3 %copy.8 = bf16[2048,2048]{0,1:T(8,128)(2,1)} copy(bf16[2048,2048]{1,0:T(8,128)(2,1)} %broadcast_select_fusion) | data formatting | bytes 16777216 | tf_op jit(solution)/shard_map/jit(_take)/select_n | solution.py:33
  50.3 20.8 %gather_fusion.1 = bf16[2048,2048]{1,0:T(8,128)(2,1)} fusion(bf16[2048,2048]{0,1:T(8,128)(2,1)} %copy.8, s32[2048]{0:T(1024)S(1)} %broadcast_clamp_fusion), kind=kCustom, calls=%fused_computation.3 | custom fusion | bytes 16785408 | tf_op jit(solution)/shard_map/jit(_take)/gather | solution.py:33
  71.1 0.0 collective-permute-done.1
  71.1 0.0 collective-permute-done
  71.2 0.1 pad_maximum_fusion
  71.3 7.8 %fusion = f32[2048,256]{1,0:T(8,128)} fusion(bf16[2048,2048]{1,0:T(8,128)(2,1)} %gather_fusion.1, pred[2048]{0:T(1024)(128)(4,1)S(1)} %compare_and_fusion, bf16[512,256]{1,0:T(8,128)(2,1)S(1)} %get-tuple-element.28, bf16[512,256]{1,0:T(8,128)(2,1)S(1)} %neg.13, bf16[512,256]{1,0:T(8,128)(2,1)S(1)} %get-tuple-element.27, bf16[512,256]{1,0:T(8,128)(2,1)S(1)} %neg.12), kind=kOutput, calls=%fused_computation.8 | convolution fusion | flops 2155872256 | bytes 11536384 | tf_op jit(solution)/shard_map/dot_general | solution.py:61
  79.1 0.6 gather_fusion.2
  79.7 0.1 broadcast_select_fusion.5
  79.8 62.6 %psum.43 = bf16[32,256]{1,0:T(8,128)(2,1)S(1)} all-reduce(bf16[32,256]{1,0:T(8,128)(2,1)S(1)} %broadcast_select_fusion.5), channel_id=1, replica_groups=mesh['sector'=16,'sub'=16] {'sub'}, use_global_device_ids=true, to_apply=%region_2.4 | all-reduce | flops 8192 | bytes 32768 | tf_op jit(solution)/shard_map/psum | solution.py:47
  142.4 33.7 %all_gather.6 = f32[512,256]{1,0:T(8,128)S(1)} all-gather(f32[32,256]{1,0:T(8,128)S(1)} %convert_element_type.35), channel_id=1, replica_groups=mesh['sector'=16,'sub'=16] {'sector'}, dimensions={0}, use_global_device_ids=true | all-gather | bytes 557056 | tf_op jit(solution)/shard_map/all_gather | solution.py:49
  176.1 0.0 copy-done
  176.1 0.3 convolution_multiply_fusion.1
  176.5 3.7 scatter_fusion
  180.1 0.0 copy-start.3
  180.1 1.8 convert.8
  182.0 0.0 copy-start.1
  182.0 1.4 collective-permute-start.2
  183.5 0.4 collective-permute-start.3
  183.9 9.4 %collective-permute-done.2 = bf16[512,256]{1,0:T(8,128)(2,1)S(1)} collective-permute-done((bf16[512,256]{1,0:T(8,128)(2,1)S(1)}, bf16[512,256]{1,0:T(8,128)(2,1)S(1)}, u32[]{:S(2)}, u32[]{:S(2)}) %collective-permute-start.2) | collective-permute-done | bytes 262176 | tf_op jit(solution)/shard_map/ppermute | solution.py:12
  193.3 0.0 collective-permute-done.3
  193.3 0.0 copy-done.3
  193.3 0.1 fusion.9
  193.5 0.0 copy-done.1
  193.5 0.2 fusion.3
  193.7 75.0 %all-reduce = (f32[256]{0:T(256)S(1)}, f32[256]{0:T(256)S(1)}) all-reduce(f32[256]{0:T(256)S(1)} %get-tuple-element.4, f32[256]{0:T(256)S(1)} %get-tuple-element.3), channel_id=1, replica_groups=mesh['sector'=16,'sub'=16] {'sector','sub'}, use_global_device_ids=true, to_apply=%region_1.2 | all-reduce | flops 512 | bytes 4096 | tf_op jit(solution)/shard_map/psum | solution.py:22
  268.7 0.2 multiply_reduce_fusion
  268.9 72.7 %psum.45 = f32[256]{0:T(256)S(1)} all-reduce(f32[256]{0:T(256)S(1)} %multiply_reduce_fusion), channel_id=1, replica_groups=mesh['sector'=16,'sub'=16] {'sector','sub'}, use_global_device_ids=true, to_apply=%region_7.9 | all-reduce | flops 256 | bytes 2048 | tf_op jit(solution)/shard_map/psum | solution.py:22
  341.7 0.2 fusion.16
  341.9 1.6 collective-permute-start.5
  343.5 3.3 collective-permute-start.4
  346.8 0.0 collective-permute-done.5
  346.9 0.1 neg.15
  346.9 7.7 %collective-permute-done.4 = bf16[512,256]{1,0:T(8,128)(2,1)S(1)} collective-permute-done((bf16[512,256]{1,0:T(8,128)(2,1)S(1)}, bf16[512,256]{1,0:T(8,128)(2,1)S(1)}, u32[]{:S(2)}, u32[]{:S(2)}) %collective-permute-start.4) | collective-permute-done | bytes 262176 | tf_op jit(solution)/shard_map/ppermute | solution.py:12
  354.6 7.8 %fusion.1 = f32[2048,256]{1,0:T(8,128)} fusion(bf16[2048,2048]{1,0:T(8,128)(2,1)} %gather_fusion.1, pred[2048]{0:T(1024)(128)(4,1)S(1)} %compare_and_fusion, bf16[512,256]{1,0:T(8,128)(2,1)S(1)} %get-tuple-element.26, bf16[512,256]{1,0:T(8,128)(2,1)S(1)} %neg.15, bf16[512,256]{1,0:T(8,128)(2,1)S(1)} %get-tuple-element.25, bf16[512,256]{1,0:T(8,128)(2,1)S(1)} %neg.14), kind=kOutput, calls=%fused_computation.9 | convolution fusion | flops 2155872256 | bytes 11536384 | tf_op jit(solution)/shard_map/dot_general | solution.py:61
  362.5 1.0 pad_maximum_fusion.1
  363.5 2.0 gather_fusion.3
  365.5 0.1 broadcast_select_fusion.4
  365.5 63.0 %psum.46 = bf16[32,256]{1,0:T(8,128)(2,1)S(1)} all-reduce(bf16[32,256]{1,0:T(8,128)(2,1)S(1)} %broadcast_select_fusion.4), channel_id=1, replica_groups=mesh['sector'=16,'sub'=16] {'sub'}, use_global_device_ids=true, to_apply=%region_8.10 | all-reduce | flops 8192 | bytes 32768 | tf_op jit(solution)/shard_map/psum | solution.py:47
  428.6 31.8 %all_gather.7 = f32[512,256]{1,0:T(8,128)S(1)} all-gather(f32[32,256]{1,0:T(8,128)S(1)} %convert_element_type.39), channel_id=1, replica_groups=mesh['sector'=16,'sub'=16] {'sector'}, dimensions={0}, use_global_device_ids=true | all-gather | bytes 557056 | tf_op jit(solution)/shard_map/all_gather | solution.py:49
  460.3 0.3 convolution_multiply_fusion
  460.7 3.7 scatter_fusion.1
  464.4 0.0 copy-start.2
  464.4 1.8 convert.9
  466.2 1.3 collective-permute-start.6
  467.5 0.2 collective-permute-start.7
  467.8 9.6 %collective-permute-done.6 = bf16[512,256]{1,0:T(8,128)(2,1)S(1)} collective-permute-done((bf16[512,256]{1,0:T(8,128)(2,1)S(1)}, bf16[512,256]{1,0:T(8,128)(2,1)S(1)}, u32[]{:S(2)}, u32[]{:S(2)}) %collective-permute-start.6) | collective-permute-done | bytes 262176 | tf_op jit(solution)/shard_map/ppermute | solution.py:12
  477.4 0.0 collective-permute-done.7
  477.4 0.0 copy-done.2
  477.4 1.1 fusion.12
  478.5 0.3 fusion.6
  478.8 76.4 %psum.47 = f32[256]{0:T(256)S(1)} all-reduce(f32[256]{0:T(256)S(1)} %fusion.6), channel_id=1, replica_groups=mesh['sector'=16,'sub'=16] {'sector','sub'}, use_global_device_ids=true, to_apply=%region_11.13 | all-reduce | flops 256 | bytes 2048 | tf_op jit(solution)/shard_map/psum | solution.py:73
  555.2 2.8 fusion.7
  (19 shorter events, 0.3 us)
Async XLA Ops:
  0.6 175.5 %copy-start = (f32[512,512]{1,0:T(8,128)S(1)}, f32[512,512]{1,0:T(8,128)}, u32[]{:S(2)}) copy-start(f32[512,512]{1,0:T(8,128)} %param.11) | copy-start | bytes 3145732
  0.6 8.9 %copy-start.5 = (s32[1,1,32]{2,1,0:T(1,128)S(1)}, s32[1,1,32]{2,1,0:T(1,128)}, u32[]{:S(2)}) copy-start(s32[1,1,32]{2,1,0:T(1,128)} %param.10) | copy-start | bytes 388
  0.7 9.0 %copy-start.4 = (s32[1,1,2048]{2,1,0:T(1,128)S(1)}, s32[1,1,2048]{2,1,0:T(1,128)}, u32[]{:S(2)}) copy-start(s32[1,1,2048]{2,1,0:T(1,128)} %param.9) | copy-start | bytes 24580
  2.1 69.0 %collective-permute-start.1 = (bf16[512,256]{1,0:T(8,128)(2,1)S(1)}, bf16[512,256]{1,0:T(8,128)(2,1)S(1)}, u32[]{:S(2)}, u32[]{:S(2)}) collective-permute-start(bf16[512,256]{1,0:T(8,128)(2,1)S(1)} %get-tuple-element.28), channel_id=1, source_target_pairs={{0,16},{16,32},{32,48},{48,64},{64,80},{80,96},{96,112},{112,128},... | collective-permute-start | bytes 786440 | tf_op jit(solution)/shard_map/ppermute | solution.py:18
  4.8 66.4 %collective-permute-start = (bf16[512,256]{1,0:T(8,128)(2,1)S(1)}, bf16[512,256]{1,0:T(8,128)(2,1)S(1)}, u32[]{:S(2)}, u32[]{:S(2)}) collective-permute-start(bf16[512,256]{1,0:T(8,128)(2,1)S(1)} %get-tuple-element.27), channel_id=1, source_target_pairs={{0,1},{1,2},{2,3},{3,4},{4,5},{5,6},{6,7},{7,8},{8,9},{9,10},{10,1... | collective-permute-start | bytes 786440 | tf_op jit(solution)/shard_map/ppermute | solution.py:12
  180.1 13.2 %copy-start.3 = (f32[2048,256]{1,0:T(8,128)S(1)}, f32[2048,256]{1,0:T(8,128)}, u32[]{:S(2)}) copy-start(f32[2048,256]{1,0:T(8,128)} %scatter_fusion) | copy-start | bytes 6291460
  182.0 11.4 %copy-start.1 = (f32[1,1,2,512,256]{4,3,2,1,0:T(8,128)S(1)}, f32[1,1,2,512,256]{4,3,2,1,0:T(8,128)}, u32[]{:S(2)}) copy-start(f32[1,1,2,512,256]{4,3,2,1,0:T(8,128)} %param.7) | copy-start | bytes 3145732
  182.0 11.3 %collective-permute-start.2 = (bf16[512,256]{1,0:T(8,128)(2,1)S(1)}, bf16[512,256]{1,0:T(8,128)(2,1)S(1)}, u32[]{:S(2)}, u32[]{:S(2)}) collective-permute-start(bf16[512,256]{1,0:T(8,128)(2,1)S(1)} %get-tuple-element.23), channel_id=1, source_target_pairs={{1,0},{2,1},{3,2},{4,3},{5,4},{6,5},{7,6},{8,7},{9,8},{10,9},{11,1... | collective-permute-start | bytes 786440 | tf_op jit(solution)/shard_map/ppermute | solution.py:12
  183.5 9.9 %collective-permute-start.3 = (bf16[512,256]{1,0:T(8,128)(2,1)S(1)}, bf16[512,256]{1,0:T(8,128)(2,1)S(1)}, u32[]{:S(2)}, u32[]{:S(2)}) collective-permute-start(bf16[512,256]{1,0:T(8,128)(2,1)S(1)} %get-tuple-element.24), channel_id=1, source_target_pairs={{0,240},{16,0},{32,16},{48,32},{64,48},{80,64},{96,80},{112,96},{1... | collective-permute-start | bytes 786440 | tf_op jit(solution)/shard_map/ppermute | solution.py:18
  341.9 4.9 collective-permute-start.5
  343.5 11.1 %collective-permute-start.4 = (bf16[512,256]{1,0:T(8,128)(2,1)S(1)}, bf16[512,256]{1,0:T(8,128)(2,1)S(1)}, u32[]{:S(2)}, u32[]{:S(2)}) collective-permute-start(bf16[512,256]{1,0:T(8,128)(2,1)S(1)} %get-tuple-element.25), channel_id=1, source_target_pairs={{0,1},{1,2},{2,3},{3,4},{4,5},{5,6},{6,7},{7,8},{8,9},{9,10},{10,1... | collective-permute-start | bytes 786440 | tf_op jit(solution)/shard_map/ppermute | solution.py:12
  464.4 13.1 %copy-start.2 = (f32[2048,256]{1,0:T(8,128)S(1)}, f32[2048,256]{1,0:T(8,128)}, u32[]{:S(2)}) copy-start(f32[2048,256]{1,0:T(8,128)} %scatter_fusion.1) | copy-start | bytes 6291460
  466.2 11.2 %collective-permute-start.6 = (bf16[512,256]{1,0:T(8,128)(2,1)S(1)}, bf16[512,256]{1,0:T(8,128)(2,1)S(1)}, u32[]{:S(2)}, u32[]{:S(2)}) collective-permute-start(bf16[512,256]{1,0:T(8,128)(2,1)S(1)} %get-tuple-element.21), channel_id=1, source_target_pairs={{1,0},{2,1},{3,2},{4,3},{5,4},{6,5},{7,6},{8,7},{9,8},{10,9},{11,1... | collective-permute-start | bytes 786440 | tf_op jit(solution)/shard_map/ppermute | solution.py:12
  467.5 9.9 %collective-permute-start.7 = (bf16[512,256]{1,0:T(8,128)(2,1)S(1)}, bf16[512,256]{1,0:T(8,128)(2,1)S(1)}, u32[]{:S(2)}, u32[]{:S(2)}) collective-permute-start(bf16[512,256]{1,0:T(8,128)(2,1)S(1)} %get-tuple-element.22), channel_id=1, source_target_pairs={{0,240},{16,0},{32,16},{48,32},{64,48},{80,64},{96,80},{112,96},{1... | collective-permute-start | bytes 786440 | tf_op jit(solution)/shard_map/ppermute | solution.py:18
where the time goes:
time: 559 us; the launch traced here: 558 us
  blocking collectives  415 us (74%)
  local copies, waits for them, and re-layouts  56.7 us (10%)
  waiting for transfers between devices  26.7 us (5%)
  other arithmetic  26.3 us (5%)
  matrix products  16.3 us (3%)
  starting transfers between devices  15.8 us (3%)
    psum x2, blocking collectives, squares(): lax.psum(jnp.sum(residual * residual, axis=(0, 1, 2, 3)), ('sector', 'sub'))  148 us
    psum x2, blocking collectives, shards(): lax.psum(partial_value.astype(jnp.bfloat16), 'sub').astype(jnp.float32)  126 us
    psum x1, blocking collectives, shards(): curvature = lax.psum(inner_sum(direction, image), ('sector', 'sub'))  76.4 us
    all_gather x2, blocking collectives, shards(): everything = lax.all_gather(sector_total, 'sector', axis=0, tiled=True)  65.5 us
    ppermute x4, waiting for transfers between devices, passed_along(): return lax.ppermute(x, axis, pairs)  26.7 us
    gather x1, local copies, waits for them, and re-layouts, shards(): jnp.take(flexibility[0, 0], slot_order, axis=0)  20.8 us
    gather x1, local copies, waits for them, and re-layouts, shards(): jnp.take(jnp.take(flexibility[0, 0], slot_order, axis=0), slot_order, axi...  20.8 us
    dot_general x2, matrix products, shards(): jnp.dot(matrix, face_stack, preferred_element_type=jnp.float32) + correction  15.6 us
  transfers between devices with their start and end apart: 8, of which 3 were waited for; matrix products, arithmetic and copies ran while one was open for 11% of the time, Pallas kernels for 0%

commit v1 on v0

v1 whole, which is shorter than its diff:
```python
import functools

import jax
import jax.numpy as jnp
from jax import lax
from jax.experimental import pallas as pl
from jax.experimental.pallas import tpu as pltpu
from jax.sharding import PartitionSpec as P

ITERS = 2
LANES = 128
MESH = pl.DeviceIdType.MESH
BF16 = jnp.bfloat16
F32 = jnp.float32

HALO_SUB, HALO_SEC, BACK_SUB, BACK_SEC, TIP_SUB, TIP_SEC = range(6)
CORNER_SUB, CORNER_SEC, COARSE_SUB, SUM_SUB, SUM_SEC = range(6, 11)
CHANNELS = 11


def dot(a, b):
    return jnp.dot(a, b, preferred_element_type=F32)


def dot_nt(a, b, precision=None):
    return lax.dot_general(
        a, b, (((1,), (1,)), ((), ())), precision=precision, preferred_element_type=F32
    )


def one_hot(condition):
    return jnp.where(condition, 1.0, 0.0).astype(BF16)


def iota(shape, axis):
    return lax.broadcasted_iota(jnp.int32, shape, axis)


def kernel(
    nsec, nsub,
    dual_hbm, matrix_hbm, order_ref, corner_ref, inverse_hbm,
    mult_ref, res_ref,
    matrix, scatter, gather, order_col, direction, rounded, spread, high, low, own, image,
    outgoing, halo_sub, halo_sec, back_sub, back_sec, tip, tip_sub, tip_sec,
    corner_pad, corner_sub, corner_sec, corner_hot, pick_hot, next_sub_hot, next_sec_hot,
    tip_hot, inverse, packed, part_sub, part_out, part_sec, coarse_out, coarse_all,
    sum_out, sum_sub, sum_mid, sum_sec,
    load_sem, index_send, index_recv, send_sem, recv_sem,
):
    rows = matrix.shape[0]
    m = rows // 4
    cases = direction.shape[1]
    nc = corner_ref.shape[1]
    share = cases // nsub
    sec, sub = lax.axis_index("sector"), lax.axis_index("sub")
    sub_next, sub_prev = lax.rem(sub + 1, nsub), lax.rem(sub + nsub - 1, nsub)
    sec_next, sec_prev = lax.rem(sec + 1, nsec), lax.rem(sec + nsec - 1, nsec)
    has_next, has_prev = sub < nsub - 1, sub > 0
    tile = min(256, m)

    barrier = pltpu.get_barrier_semaphore()

    def greet_sub(k, carry):
        pl.semaphore_signal(
            barrier, inc=1, device_id=(sec, lax.rem(sub + k, nsub)), device_id_type=MESH
        )
        return carry

    def greet_sec(k, carry):
        pl.semaphore_signal(
            barrier, inc=1, device_id=(lax.rem(sec + k, nsec), sub), device_id_type=MESH
        )
        return carry

    lax.fori_loop(1, nsub, greet_sub, 0)
    lax.fori_loop(1, nsec, greet_sec, 0)

    load_dual = pltpu.make_async_copy(dual_hbm, direction, load_sem.at[0])
    load_dual.start()
    load_inverse = [
        pltpu.make_async_copy(
            inverse_hbm.at[pl.ds(pl.multiple_of(sec * nc, nc), nc), :],
            inverse.at[pl.ds(q * nc, nc), :],
            load_sem.at[1 + q],
        )
        for q in range(3)
    ]
    for copy in load_inverse:
        copy.start()
    load_matrix = pltpu.make_async_copy(matrix_hbm, matrix, load_sem.at[4])
    load_matrix.start()

    def remote(source, target, it, channel, device):
        return pltpu.make_async_remote_copy(
            src_ref=source,
            dst_ref=target,
            send_sem=send_sem.at[it, channel],
            recv_sem=recv_sem.at[it, channel],
            device_id=device,
            device_id_type=MESH,
        )

    inverse[3 * nc :, :] = jnp.zeros((LANES - 3 * nc, inverse.shape[1]), F32)
    for it in range(ITERS):
        tip_sub[it, nc:, :] = jnp.zeros((LANES - nc, cases), BF16)
        tip_sec[it, nc:, :] = jnp.zeros((LANES - nc, cases), BF16)

        @pl.when(jnp.logical_not(has_prev))
        def _():
            halo_sub[it] = jnp.zeros((m, cases), BF16)

        @pl.when(jnp.logical_not(has_next))
        def _():
            back_sub[it] = jnp.zeros((m, cases), BF16)
            tip_sub[it, :nc, :] = jnp.zeros((nc, cases), BF16)

    corner_pad[...] = jnp.full((8, LANES), -1, jnp.int32)
    corner_pad[0:1, 0:nc] = corner_ref[...]

    @pl.when(jnp.logical_not(has_next))
    def _():
        corner_sub[...] = jnp.full((8, LANES), -1, jnp.int32)

    load_dual.wait()
    rounded[0] = direction[...].astype(BF16)

    pl.semaphore_wait(barrier, nsub - 1 + nsec - 1)

    tell_sub = pltpu.make_async_remote_copy(
        src_ref=corner_pad, dst_ref=corner_sub, send_sem=index_send.at[0],
        recv_sem=index_recv.at[0], device_id=(sec, sub_prev), device_id_type=MESH,
    )
    tell_sec = pltpu.make_async_remote_copy(
        src_ref=corner_pad, dst_ref=corner_sec, send_sem=index_send.at[1],
        recv_sem=index_recv.at[1], device_id=(sec_prev, sub), device_id_type=MESH,
    )
    pl.when(has_prev)(tell_sub.start)
    tell_sec.start()

    def halo_copies(it):
        return (
            remote(rounded.at[it, pl.ds(0, m)], halo_sub.at[it], it, HALO_SUB, (sec, sub_next)),
            remote(rounded.at[it, pl.ds(m, m)], halo_sec.at[it], it, HALO_SEC, (sec_next, sub)),
        )

    def back_copies(it):
        return (
            remote(outgoing.at[it, pl.ds(0, m)], back_sub.at[it], it, BACK_SUB, (sec, sub_prev)),
            remote(outgoing.at[it, pl.ds(m, m)], back_sec.at[it], it, BACK_SEC, (sec_prev, sub)),
        )

    def tip_copies(it):
        head = pl.ds(0, nc)
        return (
            remote(tip.at[it], tip_sub.at[it, head], it, TIP_SUB, (sec, sub_prev)),
            remote(tip.at[it], tip_sec.at[it, head], it, TIP_SEC, (sec_prev, sub)),
        )

    def send_halo(it):
        to_sub, to_sec = halo_copies(it)
        pl.when(has_next)(to_sub.start)
        to_sec.start()

    send_halo(0)

    order_row = order_ref[...]

    def build_scatter(i, carry):
        base = pl.multiple_of(i * tile, tile)
        index = iota((tile, m), 0) + base
        for block in range(4):
            hot = index == order_row[:, block * m : (block + 1) * m]
            value = -1.0 if block in (0, 2) else 1.0
            scatter[pl.ds(base, tile), block * m : (block + 1) * m] = jnp.where(
                hot, value, 0.0
            ).astype(BF16)
        return carry

    lax.fori_loop(0, rows // tile, build_scatter, 0)

    lane = iota((8, LANES), 1)
    mine = corner_pad[...]
    pl.when(has_next)(tell_sub.wait_recv)
    tell_sec.wait_recv()
    above = corner_sub[...]
    beside = corner_sec[...]
    above_rolled = pltpu.roll(above, nc, axis=1)
    beside_rolled = pltpu.roll(beside, 2 * nc, axis=1)
    own_target = jnp.where(
        mine >= 3 * m, mine - 2 * m,
        jnp.where(jnp.logical_and(mine >= m, mine < 2 * m), mine - m, -1),
    )
    above_target = jnp.where(above_rolled < m, above_rolled, -1)
    beside_target = jnp.where(
        jnp.logical_and(beside_rolled >= 2 * m, beside_rolled < 3 * m), beside_rolled - m, -1
    )
    target = jnp.where(
        lane < nc, own_target,
        jnp.where(lane < 2 * nc, above_target, jnp.where(lane < 3 * nc, beside_target, -1)),
    )

    def as_column(row):
        spread_out = jnp.broadcast_to(row.astype(F32), (LANES, LANES))
        return spread_out.T.astype(jnp.int32)

    target_col = as_column(target[0:1])[:, 0:1]
    place = iota((LANES, 2 * m), 1)
    sign = jnp.where(iota((LANES, 2 * m), 0) < nc, 1.0, -1.0)
    pick_hot[...] = jnp.where(place == target_col, sign, 0.0).astype(BF16)

    mine_first = jnp.where(lane < nc, mine, 0)
    triple = (
        mine_first + pltpu.roll(mine_first, nc, axis=1) + pltpu.roll(mine_first, 2 * nc, axis=1)
    )
    triple = jnp.where(lane < 3 * nc, triple, -1)[0:1]
    next_sub_hot[...] = one_hot(iota((m, LANES), 0) == above[0:1])
    next_sec_hot[...] = one_hot(iota((m, LANES), 0) + 2 * m == beside[0:1])

    def pack_corners(it):
        picked = dot(pick_hot[...], rounded[it])
        packed[it] = picked.T.astype(BF16)

        def share_out(k, carry):
            peer = lax.rem(sub + k, nsub)
            remote(
                packed.at[it, pl.ds(pl.multiple_of(peer * share, share), share)],
                part_sub.at[it, sub], it, CORNER_SUB, (sec, peer),
            ).start()
            return carry

        lax.fori_loop(1, nsub, share_out, 0)
        part_sub[it, sub] = packed[it, pl.ds(pl.multiple_of(sub * share, share), share), :]

    def wait_all(ref, sem):
        pltpu.make_async_copy(ref, ref, sem).wait()

    pack_corners(0)

    order_col[...] = jnp.broadcast_to(order_row.astype(F32), (LANES, rows)).T.astype(jnp.int32)

    def build_gather(i, total):
        base = pl.multiple_of(i * tile, tile)
        hot = iota((tile, LANES), 0) + base == triple
        corner_hot[pl.ds(base, tile), :] = one_hot(hot)
        column = order_col[pl.ds(base, tile), :]
        total = total + jnp.sum(jnp.where(hot, column, 0), axis=0, keepdims=True)
        cornered = dot(one_hot(hot), jnp.ones((LANES, LANES), BF16)) > 0.5
        block = base // m
        inner = jnp.logical_or(block == 1, block == 3)
        column = jnp.where(jnp.logical_and(cornered, jnp.logical_not(inner)), -1, column)[:, 0:1]
        gather[pl.ds(base, tile), :] = one_hot(iota((tile, rows), 1) == column)
        return total

    at_corner = lax.fori_loop(
        0, rows // tile, build_gather, jnp.zeros((1, LANES), jnp.int32)
    )
    tip_col = as_column(at_corner)[0:nc, 0:1]
    tip_hot[...] = one_hot(iota((nc, rows), 1) == tip_col)
    for copy in load_inverse:
        copy.wait()

    def gather_corner_sums(it):
        wait_all(part_sub.at[it, pl.ds(0, nsub - 1)], recv_sem.at[it, CORNER_SUB])
        total = part_sub[it, 0].astype(F32)
        for k in range(1, nsub):
            total = total + part_sub[it, k].astype(F32)
        total = total + pltpu.roll(total, LANES - nc, axis=1)
        part_out[it] = total

        def share_out(k, carry):
            remote(
                part_out.at[it], part_sec.at[it, sec], it, CORNER_SEC,
                (lax.rem(sec + k, nsec), sub),
            ).start()
            return carry

        lax.fori_loop(1, nsec, share_out, 0)
        part_sec[it, sec] = total

    def solve_coarse(it):
        wait_all(part_sec.at[it, pl.ds(0, nsec - 1)], recv_sem.at[it, CORNER_SEC])
        per = LANES // nc
        lanes = iota((share, LANES), 1)
        stack = []
        for first in range(0, nsec, per):
            piece = jnp.zeros((share, LANES), F32)
            for q in range(per):
                s = first + q
                a = part_sec[it, s]
                b = part_sec[it, (s - 1) % nsec]
                a = pltpu.roll(a, nc * q, axis=1) if q else a
                shift = (nc * q - 2 * nc) % LANES
                b = pltpu.roll(b, shift, axis=1) if shift else b
                inside = jnp.logical_and(lanes >= nc * q, lanes < nc * (q + 1))
                piece = jnp.where(inside, a + b, piece)
            stack.append(piece)
        corners = jnp.concatenate(stack, axis=1)
        coarse = dot_nt(corners, inverse[...], lax.Precision.HIGHEST) / nsub
        first = coarse.astype(BF16).astype(F32)
        second = (coarse - first).astype(BF16).astype(F32)
        third = coarse - first - second
        split = jnp.where(lanes < nc, first, jnp.where(lanes < 2 * nc, second, third))
        coarse_out[it] = split.astype(BF16)
        here = pl.ds(pl.multiple_of(sub * share, share), share)

        def share_out(k, carry):
            remote(
                coarse_out.at[it], coarse_all.at[it, here], it, COARSE_SUB,
                (sec, lax.rem(sub + k, nsub)),
            ).start()
            return carry

        lax.fori_loop(1, nsub, share_out, 0)
        coarse_all[it, here, :] = coarse_out[it]

    def spread_own(it):
        def body(i, carry):
            at = pl.ds(pl.multiple_of(i * tile, tile), tile)
            value = dot(scatter[at, m : 2 * m], rounded[it, :m, :])
            value += dot(scatter[at, 3 * m :], rounded[it, m:, :])
            spread[at, :] = value.astype(BF16)
            return carry

        lax.fori_loop(0, rows // tile, body, 0)

    def spread_halo(it):
        def body(i, carry):
            at = pl.ds(pl.multiple_of(i * tile, tile), tile)
            value = dot(scatter[at, 2 * m : 3 * m], halo_sec[it])
            value += dot(scatter[at, :m], halo_sub[it])
            spread[at, :] = (spread[at, :].astype(F32) + value).astype(BF16)
            return carry

        lax.fori_loop(0, rows // tile, body, 0)

    def multiply():
        def body(i, carry):
            at = pl.ds(pl.multiple_of(i * tile, tile), tile)
            value = dot(matrix[at, :], spread[...])
            top = value.astype(BF16)
            high[at, :] = top
            low[at, :] = (value - top.astype(F32)).astype(BF16)
            return carry

        lax.fori_loop(0, rows // tile, body, 0)

    def gather_out(it, half):
        def body(i, carry):
            at = pl.multiple_of(i * tile, tile)
            outgoing[it, pl.ds(at + half * m, tile), :] = dot(
                gather[pl.ds(at + 2 * half * m, tile), :], high[...]
            ).astype(BF16)
            return carry

        lax.fori_loop(0, m // tile, body, 0)

    def gather_own(half):
        def body(i, carry):
            at = pl.multiple_of(i * tile, tile)
            hot = gather[pl.ds(at + (2 * half + 1) * m, tile), :]
            own[pl.ds(at + half * m, tile), :] = dot(hot, high[...]) + dot(hot, low[...])
            return carry

        lax.fori_loop(0, m // tile, body, 0)

    def all_sum(it, values):
        pieces = []
        for value in values:
            pieces += [value[:, :LANES], value[:, LANES:]]
        pieces += [jnp.zeros((1, LANES), F32)] * (8 - len(pieces))
        sum_out[it] = jnp.concatenate(pieces, axis=0)

        def to_sub(k, carry):
            remote(
                sum_out.at[it], sum_sub.at[it, sub], it, SUM_SUB, (sec, lax.rem(sub + k, nsub))
            ).start()
            return carry

        lax.fori_loop(1, nsub, to_sub, 0)
        sum_sub[it, sub] = sum_out[it]
        wait_all(sum_sub.at[it, pl.ds(0, nsub - 1)], recv_sem.at[it, SUM_SUB])
        sum_mid[it] = jnp.sum(sum_sub[it], axis=0)

        def to_sec(k, carry):
            remote(
                sum_mid.at[it], sum_sec.at[it, sec], it, SUM_SEC, (lax.rem(sec + k, nsec), sub)
            ).start()
            return carry

        lax.fori_loop(1, nsec, to_sec, 0)
        sum_sec[it, sec] = sum_mid[it]
        wait_all(sum_sec.at[it, pl.ds(0, nsec - 1)], recv_sem.at[it, SUM_SEC])
        total = jnp.sum(sum_sec[it], axis=0)
        return [
            jnp.concatenate([total[2 * i : 2 * i + 1], total[2 * i + 1 : 2 * i + 2]], axis=1)
            for i in range(len(values))
        ]

    norm = None
    for it in range(ITERS):
        spread_own(it)
        gather_corner_sums(it)
        to_sub, to_sec = halo_copies(it)
        to_sec.wait_recv()
        pl.when(has_prev)(to_sub.wait_recv)
        spread_halo(it)
        if it == 0:
            load_matrix.wait()
        multiply()
        solve_coarse(it)
        back_to_sub, back_to_sec = back_copies(it)
        gather_out(it, 0)
        pl.when(has_prev)(back_to_sub.start)
        gather_out(it, 1)
        back_to_sec.start()
        at_tip = dot(tip_hot[...], high[...]) + dot(tip_hot[...], low[...])
        wait_all(
            coarse_all.at[it, pl.ds(0, share * (nsub - 1))], recv_sem.at[it, COARSE_SUB]
        )
        select = jnp.logical_and(
            lax.rem(iota((nc, LANES), 1), nc) == iota((nc, LANES), 0),
            iota((nc, LANES), 1) < 3 * nc,
        )
        tip[it] = (at_tip + dot_nt(one_hot(select), coarse_all[it])).astype(BF16)
        tip_to_sub, tip_to_sec = tip_copies(it)
        pl.when(has_prev)(tip_to_sub.start)
        tip_to_sec.start()
        gather_own(0)
        gather_own(1)
        for half, hot, back, rest, back_copy, tip_copy in (
            (1, next_sec_hot, back_sec, tip_sec, back_to_sec, tip_to_sec),
            (0, next_sub_hot, back_sub, tip_sub, back_to_sub, tip_to_sub),
        ):
            if half:
                back_copy.wait_recv()
                tip_copy.wait_recv()
            else:
                pl.when(has_next)(back_copy.wait_recv)
                pl.when(has_next)(tip_copy.wait_recv)
            at = pl.ds(half * m, m)
            corrected = own[at, :] + dot_nt(
                corner_hot[(2 * half + 1) * m : (2 * half + 2) * m, :], coarse_all[it]
            )
            image[at, :] = corrected - (back[it].astype(F32) + dot(hot[...], rest[it]))
        p, q = direction[...], image[...]
        curvature = jnp.sum(p * q, axis=0, keepdims=True)
        if it == 0:
            square = jnp.sum(q * q, axis=0, keepdims=True)
            start = jnp.sum(p * p, axis=0, keepdims=True)
            norm, curvature, square = all_sum(it, [start, curvature, square])
            alpha = norm / curvature
            new = norm - 2.0 * alpha * curvature + alpha * alpha * square
            beta = new / norm
            norm = new
            p = direction[...]
            residual = p - alpha * image[...]
            mult_ref[...] = alpha * p
            res_ref[...] = residual
            direction[...] = residual + beta * p
            rounded[1] = direction[...].astype(BF16)
            send_halo(1)
            pack_corners(1)
        else:
            (curvature,) = all_sum(it, [curvature])
            alpha = norm / curvature
            mult_ref[...] += alpha * direction[...]
            res_ref[...] -= alpha * image[...]

    pl.when(has_prev)(tell_sub.wait_send)
    tell_sec.wait_send()
    for it in range(ITERS):
        to_sub, to_sec = halo_copies(it)
        pl.when(has_next)(to_sub.wait_send)
        to_sec.wait_send()
        for copies in (back_copies(it), tip_copies(it)):
            pl.when(has_prev)(copies[0].wait_send)
            copies[1].wait_send()
        wait_all(part_sub.at[it, pl.ds(0, nsub - 1)], send_sem.at[it, CORNER_SUB])
        wait_all(part_sec.at[it, pl.ds(0, nsec - 1)], send_sem.at[it, CORNER_SEC])
        wait_all(
            coarse_all.at[it, pl.ds(0, share * (nsub - 1))], send_sem.at[it, COARSE_SUB]
        )
        wait_all(sum_sub.at[it, pl.ds(0, nsub - 1)], send_sem.at[it, SUM_SUB])
        wait_all(sum_sec.at[it, pl.ds(0, nsec - 1)], send_sem.at[it, SUM_SEC])


def shards(nsec, nsub, dual_load, flexibility, face_order, corner_index, coarse_inverse):
    _, _, _, m, cases = dual_load.shape
    rows = 4 * m
    nc = corner_index.shape[-1]
    share = cases // nsub
    any_space = pl.BlockSpec(memory_space=pl.ANY)
    vmem = pl.BlockSpec(memory_space=pltpu.VMEM)
    it = ITERS
    scratch = [
        ((rows, rows), BF16),
        ((rows, rows), BF16),
        ((rows, rows), BF16),
        ((rows, LANES), jnp.int32),
        ((2 * m, cases), F32),
        ((it, 2 * m, cases), BF16),
        ((rows, cases), BF16),
        ((rows, cases), BF16),
        ((rows, cases), BF16),
        ((2 * m, cases), F32),
        ((2 * m, cases), F32),
        ((it, 2 * m, cases), BF16),
        ((it, m, cases), BF16),
        ((it, m, cases), BF16),
        ((it, m, cases), BF16),
        ((it, m, cases), BF16),
        ((it, nc, cases), BF16),
        ((it, LANES, cases), BF16),
        ((it, LANES, cases), BF16),
        ((8, LANES), jnp.int32),
        ((8, LANES), jnp.int32),
        ((8, LANES), jnp.int32),
        ((rows, LANES), BF16),
        ((LANES, 2 * m), BF16),
        ((m, LANES), BF16),
        ((m, LANES), BF16),
        ((nc, rows), BF16),
        ((LANES, nsec * nc), F32),
        ((it, cases, LANES), BF16),
        ((it, nsub, share, LANES), BF16),
        ((it, share, LANES), F32),
        ((it, nsec, share, LANES), F32),
        ((it, share, LANES), BF16),
        ((it, cases, LANES), BF16),
        ((it, 8, LANES), F32),
        ((it, nsub, 8, LANES), F32),
        ((it, 8, LANES), F32),
        ((it, nsec, 8, LANES), F32),
    ]
    dma = pltpu.SemaphoreType.DMA
    out = jax.ShapeDtypeStruct((2 * m, cases), F32)
    multiplier, residual = pl.pallas_call(
        functools.partial(kernel, nsec, nsub),
        out_shape=(out, out),
        in_specs=[any_space, any_space, vmem, vmem, any_space],
        out_specs=(vmem, vmem),
        scratch_shapes=[pltpu.VMEM(shape, dtype) for shape, dtype in scratch]
        + [dma((5,)), dma((2,)), dma((2,)), dma((it, CHANNELS)), dma((it, CHANNELS))],
        compiler_params=pltpu.CompilerParams(
            collective_id=0, has_side_effects=True, vmem_limit_bytes=56 * 1024 * 1024
        ),
        cost_estimate=pl.CostEstimate(
            flops=16 * rows * rows * cases, bytes_accessed=2 * rows * rows, transcendentals=0
        ),
    )(
        dual_load.reshape(2 * m, cases),
        flexibility.reshape(rows, rows),
        face_order.reshape(1, rows),
        corner_index.reshape(1, nc),
        coarse_inverse,
    )
    return multiplier.reshape(dual_load.shape), residual.reshape(dual_load.shape)


def solution(mesh):
    spec = P("sector", "sub", None, None, None)
    return jax.shard_map(
        functools.partial(shards, mesh.shape["sector"], mesh.shape["sub"]),
        mesh=mesh,
        in_specs=(
            spec,
            P("sector", "sub", None, None),
            P("sector", "sub", None),
            P("sector", "sub", None),
            P(),
        ),
        out_specs=(spec, spec),
        check_vma=False,
    )
```

time: 559 us -> 103 us (0.18)
  blocking collectives: 415 us -> 0 us
  Pallas kernels: 0 us -> 98 us
  local copies, waits for them, and re-layouts: 56.7 us -> 4.52 us
  waiting for transfers between devices: 26.7 us -> 0 us
  other arithmetic: 26.3 us -> 0 us
  matrix products: 16.3 us -> 0 us
  starting transfers between devices: 15.8 us -> 0 us
    psum x5 -> x0, blocking collectives: 350 us -> none  [the longest x2 148 us: squares(): lax.psum(jnp.sum(residual * residual, axis=(0, 1, 2, 3)), ('sector', 'sub'))]
    pallas_call x0 -> x1, Pallas kernels: none -> 98 us  [shards(): pl.pallas_call(functools.partial(kernel, nsec, nsub), out_shape=(out, out...]
    all_gather x2 -> x0, blocking collectives: 65.5 us -> none  [shards(): everything = lax.all_gather(sector_total, 'sector', axis=0, tiled=True)]
    gather x4 -> x0, local copies, waits for them, and re-layouts: 44.2 us -> none  [the longest x1 20.8 us: shards(): jnp.take(flexibility[0, 0], slot_order, axis=0)]
    ppermute x8 -> x0, waiting for transfers between devices: 26.7 us -> none  [the longest x4 26.7 us: passed_along(): return lax.ppermute(x, axis, pairs)]
    dot_general x4 -> x0, matrix products: 16.3 us -> none  [the longest x2 15.6 us: shards(): jnp.dot(matrix, face_stack, preferred_element_type=jnp.float32) + correction]
    ppermute x8 -> x0, starting transfers between devices: 15.8 us -> none  [the longest x4 10.8 us: passed_along(): return lax.ppermute(x, axis, pairs)]
    select_n x1 -> x0, local copies, waits for them, and re-layouts: 12.3 us -> none  [shards(): jnp.take(flexibility[0, 0], slot_order, axis=0)]
  transfers between devices with their start and end apart: 8 -> 0, of which waited for: 3 -> 0; matrix products, arithmetic and copies ran while one was open for 11% -> 0% of each run, Pallas kernels for 0% -> 0%
where the time goes in v1:
time: 103 us
  Pallas kernels  98 us (95%)
  local copies, waits for them, and re-layouts  4.52 us (4%)
    pallas_call x1, Pallas kernels, shards(): pl.pallas_call(functools.partial(kernel, nsec, nsub), out_shape=(out, out...  98 us
    unnamed x2, local copies, waits for them, and re-layouts  4.52 us

profile of v1, /device:TPU:1, one launch (start us, length us, event | category | flops | bytes accessed | tf_op | source)
XLA Modules:
  0.0 103.1 jit_solution(8921209922392702606)
XLA Ops:
  0.6 98.0 %shard_map.68 = (f32[1024,256]{1,0:T(8,128)}, f32[1024,256]{1,0:T(8,128)}) custom-call(f32[1024,256]{1,0:T(8,128)} %bitcast.9, bf16[2048,2048]{1,0:T(8,128)(2,1)} %bitcast.8, s32[1,2048]{1,0:T(1,128)} %bitcast.10, s32[1,32]{1,0:T(1,128)} %bitcast.11, f32[512,512]{1,0:T(8,128)} %inverse_hbm.1), custom_call_target="tpu_custom_call" | custom-call | flops 17179869184 | bytes 8388608 | tf_op jit(solution)/shard_map/pallas_call | solution.py:537
  98.6 2.3 %copy.9 = f32[1,1,2,512,256]{4,3,2,1,0:T(8,128)} copy(f32[1,1,2,512,256]{4,3,2,1,0:T(8,128)} %bitcast.7) | data formatting | bytes 2097152
  100.9 2.3 %copy.10 = f32[1,1,2,512,256]{4,3,2,1,0:T(8,128)} copy(f32[1,1,2,512,256]{4,3,2,1,0:T(8,128)} %bitcast.6) | data formatting | bytes 2097152

commit v2 on v1

v2 whole, which is shorter than its diff:
```python
import functools

import jax
import jax.numpy as jnp
from jax import lax
from jax.experimental import pallas as pl
from jax.experimental.pallas import tpu as pltpu
from jax.sharding import PartitionSpec as P

ITERS = 2
LANES = 128
MESH = pl.DeviceIdType.MESH
BF16 = jnp.bfloat16
F32 = jnp.float32

HALO_SUB, HALO_SEC, BACK_SUB, BACK_SEC, TIP_SUB, TIP_SEC = range(6)
CORNER_SUB, CORNER_SEC, COARSE_SUB, SUM_SUB, SUM_SEC = range(6, 11)
CHANNELS = 11


def dot(a, b):
    return jnp.dot(a, b, preferred_element_type=F32)


def dot_nt(a, b, precision=None):
    return lax.dot_general(
        a, b, (((1,), (1,)), ((), ())), precision=precision, preferred_element_type=F32
    )


def one_hot(condition):
    return jnp.where(condition, 1.0, 0.0).astype(BF16)


def iota(shape, axis):
    return lax.broadcasted_iota(jnp.int32, shape, axis)


def kernel(
    nsec, nsub,
    dual_hbm, matrix_hbm, order_ref, corner_ref, inverse_hbm,
    direction_hbm, image_hbm, first_ref, turn_ref, second_ref,
    matrix, scatter, gather, direct, order_col, direction, rounded, spread, high, low, own, image,
    image_short, outgoing, halo_sub, halo_sec, back_sub, back_sec, tip, tip_sub, tip_sec,
    corner_pad, corner_sub, corner_sec, corner_hot, pick_hot, outer_hot, next_sub_hot, next_sec_hot,
    tip_hot, inverse, packed, part_sub, part_out, part_sec, coarse_out, coarse_all,
    sum_out, sum_sub, sum_mid, sum_sec,
    load_sem, store_sem, index_send, index_recv, send_sem, recv_sem,
):
    rows = matrix.shape[0]
    m = rows // 4
    cases = direction.shape[1]
    nc = corner_ref.shape[1]
    share = cases // nsub
    sec, sub = lax.axis_index("sector"), lax.axis_index("sub")
    sub_next, sub_prev = lax.rem(sub + 1, nsub), lax.rem(sub + nsub - 1, nsub)
    sec_next, sec_prev = lax.rem(sec + 1, nsec), lax.rem(sec + nsec - 1, nsec)
    has_next, has_prev = sub < nsub - 1, sub > 0
    tile = min(256, m)
    chunk = min(64, m)

    barrier = pltpu.get_barrier_semaphore()

    def greet_sub(k, carry):
        pl.semaphore_signal(
            barrier, inc=1, device_id=(sec, lax.rem(sub + k, nsub)), device_id_type=MESH
        )
        return carry

    def greet_sec(k, carry):
        pl.semaphore_signal(
            barrier, inc=1, device_id=(lax.rem(sec + k, nsec), sub), device_id_type=MESH
        )
        return carry

    lax.fori_loop(1, nsub, greet_sub, 0)
    lax.fori_loop(1, nsec, greet_sec, 0)

    load_dual = pltpu.make_async_copy(dual_hbm, direction, load_sem.at[0])
    load_dual.start()
    load_matrix = pltpu.make_async_copy(matrix_hbm, matrix, load_sem.at[1])
    load_matrix.start()
    load_inverse = []
    for place, owner in ((0, sec), (1, sec_next)):
        for q in range(3):
            copy = pltpu.make_async_copy(
                inverse_hbm.at[pl.ds(pl.multiple_of(owner * nc, nc), nc), :],
                inverse.at[pl.ds(place * LANES + q * nc, nc), :],
                load_sem.at[2 + place * 3 + q],
            )
            copy.start()
            load_inverse.append(copy)

    def remote(source, target, it, channel, device):
        return pltpu.make_async_remote_copy(
            src_ref=source,
            dst_ref=target,
            send_sem=send_sem.at[it, channel],
            recv_sem=recv_sem.at[it, channel],
            device_id=device,
            device_id_type=MESH,
        )

    def wait_all(ref, sems, it, channel):
        pltpu.make_async_copy(ref, ref, sems.at[it, channel]).wait()

    for place in range(2):
        gap = slice(place * LANES + 3 * nc, (place + 1) * LANES)
        inverse[gap, :] = jnp.zeros((LANES - 3 * nc, inverse.shape[1]), F32)
    for it in range(ITERS):

        @pl.when(jnp.logical_not(has_prev))
        def _():
            halo_sub[it] = jnp.zeros((m, cases), BF16)

        @pl.when(jnp.logical_not(has_next))
        def _():
            back_sub[it] = jnp.zeros((m, cases), BF16)
            tip_sub[it] = jnp.zeros((nc, cases), F32)

    corner_pad[...] = jnp.full((8, LANES), -1, jnp.int32)
    corner_pad[0:1, 0:nc] = corner_ref[...]

    @pl.when(jnp.logical_not(has_next))
    def _():
        corner_sub[...] = jnp.full((8, LANES), -1, jnp.int32)

    order_row = order_ref[...]

    def build_scatter(i, carry):
        base = pl.multiple_of(i * tile, tile)
        index = iota((tile, m), 0) + base
        for block in range(4):
            hot = index == order_row[:, block * m : (block + 1) * m]
            value = -1.0 if block in (0, 2) else 1.0
            scatter[pl.ds(base, tile), block * m : (block + 1) * m] = jnp.where(
                hot, value, 0.0
            ).astype(BF16)
        return carry

    lax.fori_loop(0, rows // tile, build_scatter, 0)

    lane = iota((8, LANES), 1)
    mine = corner_pad[...]
    mine_first = jnp.where(lane < nc, mine, 0)
    triple = (
        mine_first + pltpu.roll(mine_first, nc, axis=1) + pltpu.roll(mine_first, 2 * nc, axis=1)
    )
    triple = jnp.where(lane < 3 * nc, triple, -1)[0:1]
    order_col[...] = jnp.broadcast_to(order_row.astype(F32), (LANES, rows)).T.astype(jnp.int32)

    load_dual.wait()

    def round_load(i, carry):
        at = pl.ds(pl.multiple_of(i * chunk, chunk), chunk)
        rounded[0, at, :] = direction[at, :].astype(BF16)
        return carry

    lax.fori_loop(0, 2 * m // chunk, round_load, 0)

    def build_gather(i, total):
        base = pl.multiple_of(i * tile, tile)
        hot = iota((tile, LANES), 0) + base == triple
        corner_hot[pl.ds(base, tile), :] = one_hot(hot)
        column = order_col[pl.ds(base, tile), :]
        total = total + jnp.sum(jnp.where(hot, column, 0), axis=0, keepdims=True)
        cornered = dot(one_hot(hot), jnp.ones((LANES, LANES), BF16)) > 0.5
        block = base // m
        inner = jnp.logical_or(block == 1, block == 3)
        column = jnp.where(jnp.logical_and(cornered, jnp.logical_not(inner)), -1, column)[:, 0:1]
        gather[pl.ds(base, tile), :] = one_hot(iota((tile, rows), 1) == column)
        return total

    at_corner = lax.fori_loop(
        0, rows // tile, build_gather, jnp.zeros((1, LANES), jnp.int32)
    )

    def as_column(row):
        spread_out = jnp.broadcast_to(row.astype(F32), (LANES, LANES))
        return spread_out.T.astype(jnp.int32)

    tip_col = as_column(at_corner)[0:nc, 0:1]
    tip_hot[...] = one_hot(iota((nc, rows), 1) == tip_col)

    pl.semaphore_wait(barrier, nsub - 1 + nsec - 1)

    tell_sub = pltpu.make_async_remote_copy(
        src_ref=corner_pad, dst_ref=corner_sub, send_sem=index_send.at[0],
        recv_sem=index_recv.at[0], device_id=(sec, sub_prev), device_id_type=MESH,
    )
    tell_sec = pltpu.make_async_remote_copy(
        src_ref=corner_pad, dst_ref=corner_sec, send_sem=index_send.at[1],
        recv_sem=index_recv.at[1], device_id=(sec_prev, sub), device_id_type=MESH,
    )
    pl.when(has_prev)(tell_sub.start)
    tell_sec.start()

    def halo_to_sub_copy(it):
        return remote(rounded.at[it, pl.ds(0, m)], halo_sub.at[it], it, HALO_SUB, (sec, sub_next))

    def halo_to_sec_copy(it):
        return remote(rounded.at[it, pl.ds(m, m)], halo_sec.at[it], it, HALO_SEC, (sec_next, sub))

    def halo_copies(it):
        return halo_to_sub_copy(it), halo_to_sec_copy(it)

    def back_copies(it):
        return (
            remote(outgoing.at[it, pl.ds(0, m)], back_sub.at[it], it, BACK_SUB, (sec, sub_prev)),
            remote(outgoing.at[it, pl.ds(m, m)], back_sec.at[it], it, BACK_SEC, (sec_prev, sub)),
        )

    def tip_copies(it):
        return (
            remote(tip.at[it], tip_sub.at[it], it, TIP_SUB, (sec, sub_prev)),
            remote(tip.at[it], tip_sec.at[it], it, TIP_SEC, (sec_prev, sub)),
        )

    def send_halo(it):
        to_sub, to_sec = halo_copies(it)
        pl.when(has_next)(to_sub.start)
        to_sec.start()

    send_halo(0)

    load_matrix.wait()
    steps = rows // tile

    def build_direct(i, carry):
        at = pl.ds(pl.multiple_of(i * tile, tile), tile)
        direct[:, at] = dot(gather[:m, :], matrix[:, at]).astype(BF16)
        return carry

    lax.fori_loop(0, steps // 2, build_direct, 0)

    pl.when(has_next)(tell_sub.wait_recv)
    tell_sec.wait_recv()
    above = corner_sub[...]
    beside = corner_sec[...]
    above_rolled = pltpu.roll(above, nc, axis=1)
    beside_rolled = pltpu.roll(beside, 2 * nc, axis=1)
    own_target = jnp.where(
        mine >= 3 * m, mine - 2 * m,
        jnp.where(jnp.logical_and(mine >= m, mine < 2 * m), mine - m, -1),
    )
    above_target = jnp.where(above_rolled < m, above_rolled, -1)
    beside_target = jnp.where(
        jnp.logical_and(beside_rolled >= 2 * m, beside_rolled < 3 * m), beside_rolled - m, -1
    )
    target = jnp.where(
        lane < nc, own_target,
        jnp.where(lane < 2 * nc, above_target, jnp.where(lane < 3 * nc, beside_target, -1)),
    )
    target_col = as_column(target[0:1])[:, 0:1]
    place = iota((LANES, 2 * m), 1)
    sign = jnp.where(iota((LANES, 2 * m), 0) < nc, 1.0, -1.0)
    pick_hot[...] = jnp.where(place == target_col, sign, 0.0).astype(BF16)
    outer_target = jnp.where(
        mine < m, mine, jnp.where(jnp.logical_and(mine >= 2 * m, mine < 3 * m), mine - m, -1)
    )
    outer_col = as_column(outer_target[0:1])[0:nc, 0:1]
    outer_hot[...] = jnp.where(iota((nc, 2 * m), 1) == outer_col, -1.0, 0.0).astype(BF16)

    def pack_corners(it, source):
        picked = dot(pick_hot[...], source)
        packed[it] = picked.T.astype(BF16)

        def share_out(k, carry):
            peer = lax.rem(sub + k, nsub)
            remote(
                packed.at[it, pl.ds(pl.multiple_of(peer * share, share), share)],
                part_sub.at[it, sub], it, CORNER_SUB, (sec, peer),
            ).start()
            return carry

        lax.fori_loop(1, nsub, share_out, 0)
        part_sub[it, sub] = packed[it, pl.ds(pl.multiple_of(sub * share, share), share), :]

    pack_corners(0, rounded[0])

    next_sub_hot[...] = one_hot(iota((m, LANES), 0) == above[0:1])
    next_sec_hot[...] = one_hot(iota((m, LANES), 0) + 2 * m == beside[0:1])

    def gather_corner_sums(it):
        wait_all(part_sub.at[it, pl.ds(0, nsub - 1)], recv_sem, it, CORNER_SUB)
        total = part_sub[it, 0].astype(F32)
        for k in range(1, nsub):
            total = total + part_sub[it, k].astype(F32)
        total = total + pltpu.roll(total, LANES - nc, axis=1)
        part_out[it] = total

        def share_out(k, carry):
            remote(
                part_out.at[it], part_sec.at[it, sec], it, CORNER_SEC,
                (lax.rem(sec + k, nsec), sub),
            ).start()
            return carry

        lax.fori_loop(1, nsec, share_out, 0)
        part_sec[it, sec] = total

    def solve_coarse(it):
        wait_all(part_sec.at[it, pl.ds(0, nsec - 1)], recv_sem, it, CORNER_SEC)
        per = LANES // nc
        lanes = iota((share, LANES), 1)
        stack = []
        for first in range(0, nsec, per):
            piece = jnp.zeros((share, LANES), F32)
            for q in range(per):
                s = first + q
                a = part_sec[it, s]
                b = part_sec[it, (s - 1) % nsec]
                a = pltpu.roll(a, nc * q, axis=1) if q else a
                shift = (nc * q - 2 * nc) % LANES
                b = pltpu.roll(b, shift, axis=1) if shift else b
                inside = jnp.logical_and(lanes >= nc * q, lanes < nc * (q + 1))
                piece = jnp.where(inside, a + b, piece)
            stack.append(piece)
        corners = jnp.concatenate(stack, axis=1)
        coarse = dot_nt(corners, inverse[...], lax.Precision.HIGHEST) / nsub
        lanes = lax.rem(iota((share, 2 * LANES), 1), LANES)
        first = coarse.astype(BF16).astype(F32)
        second = (coarse - first).astype(BF16).astype(F32)
        third = coarse - first - second
        split = jnp.where(lanes < nc, first, jnp.where(lanes < 2 * nc, second, third))
        coarse_out[it] = split.astype(BF16)
        here = pl.ds(pl.multiple_of(sub * share, share), share)

        def share_out(k, carry):
            remote(
                coarse_out.at[it], coarse_all.at[it, here], it, COARSE_SUB,
                (sec, lax.rem(sub + k, nsub)),
            ).start()
            return carry

        lax.fori_loop(1, nsub, share_out, 0)
        coarse_all[it, here, :] = coarse_out[it]

    def wait_coarse(it):
        wait_all(coarse_all.at[it, pl.ds(0, share * (nsub - 1))], recv_sem, it, COARSE_SUB)

    def spread_own(it):
        value = dot(scatter[:, m : 2 * m], rounded[it, :m, :])
        value += dot(scatter[:, 3 * m :], rounded[it, m:, :])
        spread[...] = value.astype(BF16)

    def spread_more(block, faces):
        value = dot(scatter[:, block * m : (block + 1) * m], faces)
        spread[...] = (spread[...].astype(F32) + value).astype(BF16)

    def multiply():
        half = rows // 2
        for first in (0, half):
            at = slice(first, first + half)
            value = dot(matrix[at, :], spread[...])
            top = value.astype(BF16)
            high[at, :] = top
            low[at, :] = (value - top.astype(F32)).astype(BF16)

    def all_sum_send(it, values):
        pieces = []
        for value in values:
            pieces += [value[:, :LANES], value[:, LANES:]]
        pieces += [jnp.zeros((1, LANES), F32)] * (8 - len(pieces))
        sum_out[it] = jnp.concatenate(pieces, axis=0)

        def to_sub(k, carry):
            remote(
                sum_out.at[it], sum_sub.at[it, sub], it, SUM_SUB, (sec, lax.rem(sub + k, nsub))
            ).start()
            return carry

        lax.fori_loop(1, nsub, to_sub, 0)
        sum_sub[it, sub] = sum_out[it]

    def all_sum_pass(it):
        wait_all(sum_sub.at[it, pl.ds(0, nsub - 1)], recv_sem, it, SUM_SUB)
        sum_mid[it] = jnp.sum(sum_sub[it], axis=0)

        def to_sec(k, carry):
            remote(
                sum_mid.at[it], sum_sec.at[it, sec], it, SUM_SEC, (lax.rem(sec + k, nsec), sub)
            ).start()
            return carry

        lax.fori_loop(1, nsec, to_sec, 0)
        sum_sec[it, sec] = sum_mid[it]

    def all_sum_get(it, count):
        wait_all(sum_sec.at[it, pl.ds(0, nsec - 1)], recv_sem, it, SUM_SEC)
        total = jnp.sum(sum_sec[it], axis=0)
        return [
            jnp.concatenate([total[2 * i : 2 * i + 1], total[2 * i + 1 : 2 * i + 2]], axis=1)
            for i in range(count)
        ]

    spread_own(0)
    lax.fori_loop(steps // 2, steps, build_direct, 0)
    gather_corner_sums(0)
    for copy in load_inverse:
        copy.wait()

    alpha = beta = norm = None
    select = one_hot(
        jnp.logical_and(
            lax.rem(iota((nc, LANES), 1), nc) == iota((nc, LANES), 0),
            iota((nc, LANES), 1) < 3 * nc,
        )
    )

    def fold(x):
        return jnp.sum(x.reshape(x.shape[0] // 8, 8, cases), axis=0)

    def over_rows(x):
        return jnp.sum(x, axis=0, keepdims=True)

    for it in range(ITERS):
        last = it == ITERS - 1

        def expand(hot, place):
            lanes = slice(place * LANES, (place + 1) * LANES)
            value = dot_nt(hot, coarse_all[0, :, lanes])
            if it == 0:
                return value
            return (1.0 + beta) * value - alpha * dot_nt(hot, coarse_all[1, :, lanes])

        back_to_sub, back_to_sec = back_copies(it)
        tip_to_sub, tip_to_sec = tip_copies(it)
        halo_to_sub, halo_to_sec = halo_copies(it)
        if last:
            spread_own(it)
            solve_coarse(it)
        halo_to_sec.wait_recv()
        spread_more(2, halo_sec[it])
        if last:
            wait_coarse(it)
        pl.when(has_prev)(halo_to_sub.wait_recv)
        spread_more(0, halo_sub[it])
        if not last:
            outgoing[it, :m, :] = dot(direct[...], spread[...]).astype(BF16)
            pl.when(has_prev)(back_to_sub.start)
        multiply()
        at_tip = dot(tip_hot[...], high[...]) + dot(tip_hot[...], low[...])
        tip[it] = at_tip
        if last:
            def weigh(i, total):
                here = pl.ds(pl.multiple_of(i * chunk, chunk), chunk)
                value = high[here, :].astype(F32) + low[here, :].astype(F32)
                return total + fold(spread[here, :].astype(F32) * value)

            p_q = over_rows(
                lax.fori_loop(0, rows // chunk, weigh, jnp.zeros((8, cases), F32))
            )
            faces = dot(outer_hot[:, :m], halo_sub[it]) + dot(outer_hot[:, m:], halo_sec[it])
            faces += dot(pick_hot[:nc, :], rounded[it])
            all_sum_send(it, [p_q + over_rows(faces * expand(select, 0))])
            outgoing[it, :m, :] = dot(gather[:m, :], high[...]).astype(BF16)
            pl.when(has_prev)(back_to_sub.start)
        outgoing[it, m:, :] = dot(gather[2 * m : 3 * m, :], high[...]).astype(BF16)
        back_to_sec.start()
        pl.when(has_prev)(tip_to_sub.start)
        tip_to_sec.start()
        if not last:
            solve_coarse(it)
        for half in (1, 0):
            block = 2 * half + 1
            hot = gather[block * m : (block + 1) * m, :]
            own[half * m : (half + 1) * m, :] = dot(hot, high[...]) + dot(hot, low[...])
        if last:
            all_sum_pass(it)
        else:
            wait_coarse(it)
        p_q = jnp.zeros((8, cases), F32)
        q_q = jnp.zeros((8, cases), F32)
        p_p = jnp.zeros((8, cases), F32)
        for half, hot, back, rest, back_copy, tip_copy in (
            (1, next_sec_hot, back_sec, tip_sec, back_to_sec, tip_to_sec),
            (0, next_sub_hot, back_sub, tip_sub, back_to_sub, tip_to_sub),
        ):
            block = 2 * half + 1
            at = slice(half * m, (half + 1) * m)
            own[at, :] = own[at, :] + expand(corner_hot[block * m : (block + 1) * m, :], 0)
            if half:
                tip_copy.wait_recv()
            else:
                pl.when(has_next)(tip_copy.wait_recv)
            value = (rest[it] + expand(select, half)).astype(BF16)
            value = jnp.concatenate([value, jnp.zeros((LANES - nc, cases), BF16)], axis=0)
            own[at, :] = own[at, :] - dot(hot[...], value)
            if half:
                back_copy.wait_recv()
            else:
                pl.when(has_next)(back_copy.wait_recv)

            def finish(i, sums, half=half, back=back):
                base = pl.multiple_of(i * chunk, chunk)
                here = pl.ds(base + half * m, chunk)
                q = own[here, :] - back[it, pl.ds(base, chunk), :].astype(F32)
                image[here, :] = q
                if last:
                    return sums
                p = direction[here, :]
                image_short[here, :] = q.astype(BF16)
                p_q, q_q, p_p = sums
                return p_q + fold(p * q), q_q + fold(q * q), p_p + fold(p * p)

            p_q, q_q, p_p = lax.fori_loop(0, m // chunk, finish, (p_q, q_q, p_p))
        if not last:
            all_sum_send(it, [over_rows(p_p), over_rows(p_q), over_rows(q_q)])
            pack_corners(1, image_short[...])
            all_sum_pass(it)
            gather_corner_sums(1)
            norm, curvature, square = all_sum_get(it, 3)
            alpha = norm / curvature
            new = norm - 2.0 * alpha * curvature + alpha * alpha * square
            beta = new / norm
            norm = new
            for half in range(2):

                def turn(i, carry, half=half):
                    here = pl.ds(pl.multiple_of(i * chunk + half * m, chunk), chunk)
                    p = direction[here, :]
                    p = p - alpha * image[here, :] + beta * p
                    direction[here, :] = p
                    rounded[1, here, :] = p.astype(BF16)
                    return carry

                lax.fori_loop(0, m // chunk, turn, 0)
                if half:
                    halo_to_sec_copy(1).start()
                else:
                    pl.when(has_next)(halo_to_sub_copy(1).start)
            store_direction = pltpu.make_async_copy(direction, direction_hbm, store_sem.at[0])
            store_direction.start()
        else:
            store_image = pltpu.make_async_copy(image, image_hbm, store_sem.at[1])
            store_image.start()
            (curvature,) = all_sum_get(it, 1)
            first_ref[...] = alpha
            turn_ref[...] = beta
            second_ref[...] = norm / curvature

    store_direction.wait()
    store_image.wait()
    pl.when(has_prev)(tell_sub.wait_send)
    tell_sec.wait_send()
    for it in range(ITERS):
        to_sub, to_sec = halo_copies(it)
        pl.when(has_next)(to_sub.wait_send)
        to_sec.wait_send()
        for copies in (back_copies(it), tip_copies(it)):
            pl.when(has_prev)(copies[0].wait_send)
            copies[1].wait_send()
        wait_all(part_sub.at[it, pl.ds(0, nsub - 1)], send_sem, it, CORNER_SUB)
        wait_all(part_sec.at[it, pl.ds(0, nsec - 1)], send_sem, it, CORNER_SEC)
        wait_all(coarse_all.at[it, pl.ds(0, share * (nsub - 1))], send_sem, it, COARSE_SUB)
        wait_all(sum_sub.at[it, pl.ds(0, nsub - 1)], send_sem, it, SUM_SUB)
        wait_all(sum_sec.at[it, pl.ds(0, nsec - 1)], send_sem, it, SUM_SEC)


def shards(nsec, nsub, dual_load, flexibility, face_order, corner_index, coarse_inverse):
    _, _, _, m, cases = dual_load.shape
    rows = 4 * m
    nc = corner_index.shape[-1]
    share = cases // nsub
    any_space = pl.BlockSpec(memory_space=pl.ANY)
    vmem = pl.BlockSpec(memory_space=pltpu.VMEM)
    it = ITERS
    scratch = [
        ((rows, rows), BF16),
        ((rows, rows), BF16),
        ((rows, rows), BF16),
        ((m, rows), BF16),
        ((rows, LANES), jnp.int32),
        ((2 * m, cases), F32),
        ((it, 2 * m, cases), BF16),
        ((rows, cases), BF16),
        ((rows, cases), BF16),
        ((rows, cases), BF16),
        ((2 * m, cases), F32),
        ((2 * m, cases), F32),
        ((2 * m, cases), BF16),
        ((it, 2 * m, cases), BF16),
        ((it, m, cases), BF16),
        ((it, m, cases), BF16),
        ((it, m, cases), BF16),
        ((it, m, cases), BF16),
        ((it, nc, cases), F32),
        ((it, nc, cases), F32),
        ((it, nc, cases), F32),
        ((8, LANES), jnp.int32),
        ((8, LANES), jnp.int32),
        ((8, LANES), jnp.int32),
        ((rows, LANES), BF16),
        ((LANES, 2 * m), BF16),
        ((nc, 2 * m), BF16),
        ((m, LANES), BF16),
        ((m, LANES), BF16),
        ((nc, rows), BF16),
        ((2 * LANES, nsec * nc), F32),
        ((it, cases, LANES), BF16),
        ((it, nsub, share, LANES), BF16),
        ((it, share, LANES), F32),
        ((it, nsec, share, LANES), F32),
        ((it, share, 2 * LANES), BF16),
        ((it, cases, 2 * LANES), BF16),
        ((it, 8, LANES), F32),
        ((it, nsub, 8, LANES), F32),
        ((it, 8, LANES), F32),
        ((it, nsec, 8, LANES), F32),
    ]
    dma = pltpu.SemaphoreType.DMA
    out = jax.ShapeDtypeStruct((2 * m, cases), F32)
    row = jax.ShapeDtypeStruct((1, cases), F32)
    direction, image, first, turn, second = pl.pallas_call(
        functools.partial(kernel, nsec, nsub),
        out_shape=(out, out, row, row, row),
        in_specs=[any_space, any_space, vmem, vmem, any_space],
        out_specs=(any_space, any_space, vmem, vmem, vmem),
        scratch_shapes=[pltpu.VMEM(shape, dtype) for shape, dtype in scratch]
        + [dma((8,)), dma((2,)), dma((2,)), dma((2,)), dma((it, CHANNELS)), dma((it, CHANNELS))],
        compiler_params=pltpu.CompilerParams(
            collective_id=0, has_side_effects=True, vmem_limit_bytes=56 * 1024 * 1024
        ),
        cost_estimate=pl.CostEstimate(
            flops=16 * rows * rows * cases, bytes_accessed=2 * rows * rows, transcendentals=0
        ),
    )(
        dual_load.reshape(2 * m, cases),
        flexibility.reshape(rows, rows),
        face_order.reshape(1, rows),
        corner_index.reshape(1, nc),
        coarse_inverse,
    )
    direction, image = direction.reshape(dual_load.shape), image.reshape(dual_load.shape)
    first, turn, second = first.reshape(cases), turn.reshape(cases), second.reshape(cases)
    multiplier = first * dual_load + second * direction
    residual = direction - turn * dual_load - second * image
    return multiplier, residual


def solution(mesh):
    spec = P("sector", "sub", None, None, None)
    return jax.shard_map(
        functools.partial(shards, mesh.shape["sector"], mesh.shape["sub"]),
        mesh=mesh,
        in_specs=(
            spec,
            P("sector", "sub", None, None),
            P("sector", "sub", None),
            P("sector", "sub", None),
            P(),
        ),
        out_specs=(spec, spec),
        check_vma=False,
    )
```

time: 103 us -> 88.5 us (0.86)
  Pallas kernels: 98 us -> 84.6 us
  local copies, waits for them, and re-layouts: 4.52 us -> 0.01 us
  other arithmetic: 0 us -> 3.11 us
    pallas_call x1, Pallas kernels: 98 us -> 84.6 us  [shards(): pl.pallas_call(functools.partial(kernel, nsec, nsub), out_shape=(out, out...]
    unnamed x2, local copies, waits for them, and re-layouts: 4.52 us -> 0.01 us
    sub x0 -> x1, other arithmetic: none -> 3.11 us  [shards(): residual = direction - turn * dual_load - second * image]
where the time goes in v2:
time: 88.5 us; the launch traced here: 88.3 us
  Pallas kernels  84.6 us (96%)
  other arithmetic  3.11 us (4%)
    pallas_call x1, Pallas kernels, shards(): pl.pallas_call(functools.partial(kernel, nsec, nsub), out_shape=(out, out...  84.6 us
    sub x1, other arithmetic, shards(): residual = direction - turn * dual_load - second * image  3.11 us

profile of v2, /device:TPU:1, one launch (start us, length us, event | category | flops | bytes accessed | tf_op | source)
XLA Modules:
  0.0 88.3 jit_solution(5464990255521965518)
XLA Ops:
  0.6 0.0 copy-start
  0.6 84.6 %shard_map.68 = (f32[1024,256]{1,0:T(8,128)}, f32[1024,256]{1,0:T(8,128)}, f32[1,256]{1,0:T(1,128)}, f32[1,256]{1,0:T(1,128)}, f32[1,256]{1,0:T(1,128)}) custom-call(f32[1024,256]{1,0:T(8,128)} %bitcast.9, bf16[2048,2048]{1,0:T(8,128)(2,1)} %bitcast.15, s32[1,2048]{1,0:T(1,128)} %bitcast.16, s32[1,32]{1,0:T(1,128)} %bitcast.17, f32[512,512]{1,0:T(8,128)} %inverse_hbm.1), custom_call_target="tpu_custom_call" | custom-call | flops 17179869184 | bytes 8388608 | tf_op jit(solution)/shard_map/pallas_call | solution.py:615
  85.2 0.0 copy-done
  85.2 3.1 %multiply_subtract_fusion = (f32[1,1,2,512,256]{4,3,2,1,0:T(8,128)}, f32[1,1,2,512,256]{4,3,2,1,0:T(8,128)}) fusion(f32[1,1,2,512,256]{4,3,2,1,0:T(8,128)} %bitcast.11, f32[1,1,2,512,256]{4,3,2,1,0:T(8,128)} %bitcast.10, f32[1,1,2,512,256]{4,3,2,1,0:T(8,128)S(1)} %copy-done, f32[256]{0:T(256)} %bitcast.13, f32[256]{0:T(256)} %bitcast.14, f32[256]{0:T(256)} %bitcast.12), kind=kLoop, calls=%fused_computation | loop fusion | flops 1835008 | bytes 5245952 | tf_op jit(solution)/shard_map/sub | solution.py:638
Async XLA Ops:
  0.6 84.6 %copy-start = (f32[1,1,2,512,256]{4,3,2,1,0:T(8,128)S(1)}, f32[1,1,2,512,256]{4,3,2,1,0:T(8,128)}, u32[]{:S(2)}) copy-start(f32[1,1,2,512,256]{4,3,2,1,0:T(8,128)} %param.5) | copy-start | bytes 3145732

commit v3 on v2

--- a/solution.py
+++ b/solution.py
@@ -14,7 +14,7 @@
 F32 = jnp.float32
 
 HALO_SUB, HALO_SEC, BACK_SUB, BACK_SEC, TIP_SUB, TIP_SEC = range(6)
-CORNER_SUB, CORNER_SEC, COARSE_SUB, SUM_SUB, SUM_SEC = range(6, 11)
+CORNER_SUB, CORNER_SEC, COARSE_SUB, SUM_FIRST, SUM_SECOND = range(6, 11)
 CHANNELS = 11
 
 
@@ -40,18 +40,19 @@
     nsec, nsub,
     dual_hbm, matrix_hbm, order_ref, corner_ref, inverse_hbm,
     direction_hbm, image_hbm, first_ref, turn_ref, second_ref,
-    matrix, scatter, gather, direct, order_col, direction, rounded, spread, high, low, own, image,
+    matrix, scatter, gather, order_col, direction, rounded, spread, high, low, own, image,
     image_short, outgoing, halo_sub, halo_sec, back_sub, back_sec, tip, tip_sub, tip_sec,
     corner_pad, corner_sub, corner_sec, corner_hot, pick_hot, outer_hot, next_sub_hot, next_sec_hot,
     tip_hot, inverse, packed, part_sub, part_out, part_sec, coarse_out, coarse_all,
-    sum_out, sum_sub, sum_mid, sum_sec,
+    sum_out, sum_first, sum_mid, sum_second,
     load_sem, store_sem, index_send, index_recv, send_sem, recv_sem,
 ):
     rows = matrix.shape[0]
     m = rows // 4
     cases = direction.shape[1]
     nc = corner_ref.shape[1]
-    share = cases // nsub
+    share = cases // (nsub // 2)
+    half_share = share // 2
     sec, sub = lax.axis_index("sector"), lax.axis_index("sub")
     sub_next, sub_prev = lax.rem(sub + 1, nsub), lax.rem(sub + nsub - 1, nsub)
     sec_next, sec_prev = lax.rem(sec + 1, nsec), lax.rem(sec + nsec - 1, nsec)
@@ -61,20 +62,49 @@
 
     barrier = pltpu.get_barrier_semaphore()
 
-    def greet_sub(k, carry):
-        pl.semaphore_signal(
-            barrier, inc=1, device_id=(sec, lax.rem(sub + k, nsub)), device_id_type=MESH
-        )
-        return carry
-
-    def greet_sec(k, carry):
-        pl.semaphore_signal(
-            barrier, inc=1, device_id=(lax.rem(sec + k, nsec), sub), device_id_type=MESH
-        )
-        return carry
-
-    lax.fori_loop(1, nsub, greet_sub, 0)
-    lax.fori_loop(1, nsec, greet_sec, 0)
+    turns = nsec // 4
+    depth = nsub // 2
+
+    def ring(step, size):
+        return min(step, size - step)
+
+    def reach(ahead, aside):
+        low, across = aside // 2, aside % 2
+        over, along = ahead // (2 * turns), ahead // 2 % turns
+        return ring(low, depth) + 2 * across + over + ring(along, turns) + 0.5 * (ahead % 2)
+
+    sub_steps = sorted(range(1, nsub), key=lambda k: -reach(0, k))
+    sec_steps = sorted(range(1, nsec), key=lambda k: -reach(k, 0))
+    z, y_hi = sub // 2, lax.rem(sub, 2)
+    y_lo, x, core = sec // (2 * turns), lax.rem(sec // 2, turns), lax.rem(sec, 2)
+    first_steps = sorted(
+        ((a, b) for a in range(depth) for b in range(2) if a or b),
+        key=lambda step: -ring(step[0], depth) - 0.5 * step[1],
+    )
+    second_steps = sorted(
+        (
+            (a, b, c) for a in range(2) for b in range(turns) for c in range(2) if a or b or c
+        ),
+        key=lambda step: -step[0] - ring(step[1], turns) - 2 * step[2],
+    )
+
+    def first_peer(step):
+        a, b = step
+        return (sec + lax.rem(core + b, 2) - core, lax.rem(z + a, depth) * 2 + y_hi)
+
+    def second_peer(step):
+        a, b, c = step
+        place = lax.rem(y_lo + a, 2) * turns + lax.rem(x + b, turns)
+        return (place * 2 + core, z * 2 + lax.rem(y_hi + c, 2))
+
+    first_slot = z * 2 + core
+    second_slot = (y_lo * turns + x) * 2 + y_hi
+    peers = [(sec, lax.rem(sub + k, nsub)) for k in sub_steps]
+    peers += [(lax.rem(sec + k, nsec), sub) for k in sec_steps]
+    peers += [first_peer(step) for step in first_steps if step[0] and step[1]]
+    peers += [second_peer(step) for step in second_steps if (step[0] or step[1]) and step[2]]
+    for peer in peers:
+        pl.semaphore_signal(barrier, inc=1, device_id=peer, device_id_type=MESH)
 
     load_dual = pltpu.make_async_copy(dual_hbm, direction, load_sem.at[0])
     load_dual.start()
@@ -171,18 +201,10 @@
         gather[pl.ds(base, tile), :] = one_hot(iota((tile, rows), 1) == column)
         return total
 
-    at_corner = lax.fori_loop(
-        0, rows // tile, build_gather, jnp.zeros((1, LANES), jnp.int32)
-    )
-
-    def as_column(row):
-        spread_out = jnp.broadcast_to(row.astype(F32), (LANES, LANES))
-        return spread_out.T.astype(jnp.int32)
-
-    tip_col = as_column(at_corner)[0:nc, 0:1]
-    tip_hot[...] = one_hot(iota((nc, rows), 1) == tip_col)
-
-    pl.semaphore_wait(barrier, nsub - 1 + nsec - 1)
+    steps = rows // tile
+    ahead = steps // 2
+    at_corner = lax.fori_loop(0, ahead, build_gather, jnp.zeros((1, LANES), jnp.int32))
+    pl.semaphore_wait(barrier, len(peers))
 
     tell_sub = pltpu.make_async_remote_copy(
         src_ref=corner_pad, dst_ref=corner_sub, send_sem=index_send.at[0],
@@ -222,16 +244,22 @@
         to_sec.start()
 
     send_halo(0)
-
-    load_matrix.wait()
-    steps = rows // tile
-
-    def build_direct(i, carry):
-        at = pl.ds(pl.multiple_of(i * tile, tile), tile)
-        direct[:, at] = dot(gather[:m, :], matrix[:, at]).astype(BF16)
-        return carry
-
-    lax.fori_loop(0, steps // 2, build_direct, 0)
+    at_corner = lax.fori_loop(ahead, steps, build_gather, at_corner)
+
+    def as_column(row):
+        spread_out = jnp.broadcast_to(row.astype(F32), (LANES, LANES))
+        return spread_out.T.astype(jnp.int32)
+
+    tip_col = as_column(at_corner)[0:nc, 0:1]
+    tip_hot[...] = one_hot(iota((nc, rows), 1) == tip_col)
+
+
+    def spread_own(it):
+        value = dot(scatter[:, m : 2 * m], rounded[it, :m, :])
+        value += dot(scatter[:, 3 * m :], rounded[it, m:, :])
+        spread[...] = value.astype(BF16)
+
+    spread_own(0)
 
     pl.when(has_next)(tell_sub.wait_recv)
     tell_sec.wait_recv()
@@ -265,16 +293,13 @@
         picked = dot(pick_hot[...], source)
         packed[it] = picked.T.astype(BF16)
 
-        def share_out(k, carry):
+        for k in sub_steps:
             peer = lax.rem(sub + k, nsub)
             remote(
-                packed.at[it, pl.ds(pl.multiple_of(peer * share, share), share)],
+                packed.at[it, pl.ds(pl.multiple_of(peer // 2 * share, share), share)],
                 part_sub.at[it, sub], it, CORNER_SUB, (sec, peer),
             ).start()
-            return carry
-
-        lax.fori_loop(1, nsub, share_out, 0)
-        part_sub[it, sub] = packed[it, pl.ds(pl.multiple_of(sub * share, share), share), :]
+        part_sub[it, sub] = packed[it, pl.ds(pl.multiple_of(z * share, share), share), :]
 
     pack_corners(0, rounded[0])
 
@@ -287,36 +312,40 @@
         for k in range(1, nsub):
             total = total + part_sub[it, k].astype(F32)
         total = total + pltpu.roll(total, LANES - nc, axis=1)
+        lanes = iota((half_share, LANES), 1)
+        even = lax.rem(lanes // nc, 2) == 0
+        total = jnp.where(even, total[:half_share], pltpu.roll(total[half_share:], nc, axis=1))
         part_out[it] = total
 
-        def share_out(k, carry):
+        for k in sec_steps:
             remote(
                 part_out.at[it], part_sec.at[it, sec], it, CORNER_SEC,
                 (lax.rem(sec + k, nsec), sub),
             ).start()
-            return carry
-
-        lax.fori_loop(1, nsec, share_out, 0)
         part_sec[it, sec] = total
 
     def solve_coarse(it):
         wait_all(part_sec.at[it, pl.ds(0, nsec - 1)], recv_sem, it, CORNER_SEC)
         per = LANES // nc
-        lanes = iota((share, LANES), 1)
-        stack = []
-        for first in range(0, nsec, per):
-            piece = jnp.zeros((share, LANES), F32)
-            for q in range(per):
-                s = first + q
-                a = part_sec[it, s]
-                b = part_sec[it, (s - 1) % nsec]
-                a = pltpu.roll(a, nc * q, axis=1) if q else a
-                shift = (nc * q - 2 * nc) % LANES
-                b = pltpu.roll(b, shift, axis=1) if shift else b
-                inside = jnp.logical_and(lanes >= nc * q, lanes < nc * (q + 1))
-                piece = jnp.where(inside, a + b, piece)
-            stack.append(piece)
-        corners = jnp.concatenate(stack, axis=1)
+        lanes = iota((half_share, LANES), 1)
+
+        def turned(value, shift):
+            return pltpu.roll(value, shift % LANES, axis=1) if shift % LANES else value
+
+        halves = []
+        for half in range(2):
+            stack = []
+            for first in range(0, nsec, per):
+                piece = jnp.zeros((half_share, LANES), F32)
+                for q in range(per):
+                    s = first + q
+                    here = turned(part_sec[it, s], nc * (q - half))
+                    before = turned(part_sec[it, (s - 1) % nsec], nc * (q - 2 - half))
+                    inside = jnp.logical_and(lanes >= nc * q, lanes < nc * (q + 1))
+                    piece = jnp.where(inside, here + before, piece)
+                stack.append(piece)
+            halves.append(jnp.concatenate(stack, axis=1))
+        corners = jnp.concatenate(halves, axis=0)
         coarse = dot_nt(corners, inverse[...], lax.Precision.HIGHEST) / nsub
         lanes = lax.rem(iota((share, 2 * LANES), 1), LANES)
         first = coarse.astype(BF16).astype(F32)
@@ -324,25 +353,17 @@
         third = coarse - first - second
         split = jnp.where(lanes < nc, first, jnp.where(lanes < 2 * nc, second, third))
         coarse_out[it] = split.astype(BF16)
-        here = pl.ds(pl.multiple_of(sub * share, share), share)
-
-        def share_out(k, carry):
+        here = pl.ds(pl.multiple_of(z * share, share), share)
+
+        for k in sorted(range(1, depth), key=lambda k: -ring(k, depth)):
             remote(
                 coarse_out.at[it], coarse_all.at[it, here], it, COARSE_SUB,
-                (sec, lax.rem(sub + k, nsub)),
+                (sec, lax.rem(z + k, depth) * 2 + y_hi),
             ).start()
-            return carry
-
-        lax.fori_loop(1, nsub, share_out, 0)
         coarse_all[it, here, :] = coarse_out[it]
 
     def wait_coarse(it):
-        wait_all(coarse_all.at[it, pl.ds(0, share * (nsub - 1))], recv_sem, it, COARSE_SUB)
-
-    def spread_own(it):
-        value = dot(scatter[:, m : 2 * m], rounded[it, :m, :])
-        value += dot(scatter[:, 3 * m :], rounded[it, m:, :])
-        spread[...] = value.astype(BF16)
+        wait_all(coarse_all.at[it, pl.ds(0, share * (depth - 1))], recv_sem, it, COARSE_SUB)
 
     def spread_more(block, faces):
         value = dot(scatter[:, block * m : (block + 1) * m], faces)
@@ -364,39 +385,29 @@
         pieces += [jnp.zeros((1, LANES), F32)] * (8 - len(pieces))
         sum_out[it] = jnp.concatenate(pieces, axis=0)
 
-        def to_sub(k, carry):
+        for step in first_steps:
             remote(
-                sum_out.at[it], sum_sub.at[it, sub], it, SUM_SUB, (sec, lax.rem(sub + k, nsub))
+                sum_out.at[it], sum_first.at[it, first_slot], it, SUM_FIRST, first_peer(step)
             ).start()
-            return carry
-
-        lax.fori_loop(1, nsub, to_sub, 0)
-        sum_sub[it, sub] = sum_out[it]
+        sum_first[it, first_slot] = sum_out[it]
 
     def all_sum_pass(it):
-        wait_all(sum_sub.at[it, pl.ds(0, nsub - 1)], recv_sem, it, SUM_SUB)
-        sum_mid[it] = jnp.sum(sum_sub[it], axis=0)
-
-        def to_sec(k, carry):
+        wait_all(sum_first.at[it, pl.ds(0, len(first_steps))], recv_sem, it, SUM_FIRST)
+        sum_mid[it] = jnp.sum(sum_first[it], axis=0)
+        for step in second_steps:
             remote(
-                sum_mid.at[it], sum_sec.at[it, sec], it, SUM_SEC, (lax.rem(sec + k, nsec), sub)
+                sum_mid.at[it], sum_second.at[it, second_slot], it, SUM_SECOND, second_peer(step)
             ).start()
-            return carry
-
-        lax.fori_loop(1, nsec, to_sec, 0)
-        sum_sec[it, sec] = sum_mid[it]
+        sum_second[it, second_slot] = sum_mid[it]
 
     def all_sum_get(it, count):
-        wait_all(sum_sec.at[it, pl.ds(0, nsec - 1)], recv_sem, it, SUM_SEC)
-        total = jnp.sum(sum_sec[it], axis=0)
+        wait_all(sum_second.at[it, pl.ds(0, len(second_steps))], recv_sem, it, SUM_SECOND)
+        total = jnp.sum(sum_second[it], axis=0)
         return [
             jnp.concatenate([total[2 * i : 2 * i + 1], total[2 * i + 1 : 2 * i + 2]], axis=1)
             for i in range(count)
         ]
 
-    spread_own(0)
-    lax.fori_loop(steps // 2, steps, build_direct, 0)
-    gather_corner_sums(0)
     for copy in load_inverse:
         copy.wait()
 
@@ -437,8 +448,8 @@
         pl.when(has_prev)(halo_to_sub.wait_recv)
         spread_more(0, halo_sub[it])
         if not last:
-            outgoing[it, :m, :] = dot(direct[...], spread[...]).astype(BF16)
-            pl.when(has_prev)(back_to_sub.start)
+            gather_corner_sums(0)
+            load_matrix.wait()
         multiply()
         at_tip = dot(tip_hot[...], high[...]) + dot(tip_hot[...], low[...])
         tip[it] = at_tip
@@ -454,8 +465,8 @@
             faces = dot(outer_hot[:, :m], halo_sub[it]) + dot(outer_hot[:, m:], halo_sec[it])
             faces += dot(pick_hot[:nc, :], rounded[it])
             all_sum_send(it, [p_q + over_rows(faces * expand(select, 0))])
-            outgoing[it, :m, :] = dot(gather[:m, :], high[...]).astype(BF16)
-            pl.when(has_prev)(back_to_sub.start)
+        outgoing[it, :m, :] = dot(gather[:m, :], high[...]).astype(BF16)
+        pl.when(has_prev)(back_to_sub.start)
         outgoing[it, m:, :] = dot(gather[2 * m : 3 * m, :], high[...]).astype(BF16)
         back_to_sec.start()
         pl.when(has_prev)(tip_to_sub.start)
@@ -553,16 +564,16 @@
             copies[1].wait_send()
         wait_all(part_sub.at[it, pl.ds(0, nsub - 1)], send_sem, it, CORNER_SUB)
         wait_all(part_sec.at[it, pl.ds(0, nsec - 1)], send_sem, it, CORNER_SEC)
-        wait_all(coarse_all.at[it, pl.ds(0, share * (nsub - 1))], send_sem, it, COARSE_SUB)
-        wait_all(sum_sub.at[it, pl.ds(0, nsub - 1)], send_sem, it, SUM_SUB)
-        wait_all(sum_sec.at[it, pl.ds(0, nsec - 1)], send_sem, it, SUM_SEC)
+        wait_all(coarse_all.at[it, pl.ds(0, share * (depth - 1))], send_sem, it, COARSE_SUB)
+        wait_all(sum_first.at[it, pl.ds(0, len(first_steps))], send_sem, it, SUM_FIRST)
+        wait_all(sum_second.at[it, pl.ds(0, len(second_steps))], send_sem, it, SUM_SECOND)
 
 
 def shards(nsec, nsub, dual_load, flexibility, face_order, corner_index, coarse_inverse):
     _, _, _, m, cases = dual_load.shape
     rows = 4 * m
     nc = corner_index.shape[-1]
-    share = cases // nsub
+    share = cases // (nsub // 2)
     any_space = pl.BlockSpec(memory_space=pl.ANY)
     vmem = pl.BlockSpec(memory_space=pltpu.VMEM)
     it = ITERS
@@ -570,7 +581,6 @@
         ((rows, rows), BF16),
         ((rows, rows), BF16),
         ((rows, rows), BF16),
-        ((m, rows), BF16),
         ((rows, LANES), jnp.int32),
         ((2 * m, cases), F32),
         ((it, 2 * m, cases), BF16),
@@ -600,14 +610,14 @@
         ((2 * LANES, nsec * nc), F32),
         ((it, cases, LANES), BF16),
         ((it, nsub, share, LANES), BF16),
-        ((it, share, LANES), F32),
-        ((it, nsec, share, LANES), F32),
+        ((it, share // 2, LANES), F32),
+        ((it, nsec, share // 2, LANES), F32),
         ((it, share, 2 * LANES), BF16),
         ((it, cases, 2 * LANES), BF16),
         ((it, 8, LANES), F32),
-        ((it, nsub, 8, LANES), F32),
+        ((it, nsub // 2 * 2, 8, LANES), F32),
         ((it, 8, LANES), F32),
-        ((it, nsec, 8, LANES), F32),
+        ((it, nsec // 4 * 4, 8, LANES), F32),
     ]
     dma = pltpu.SemaphoreType.DMA
     out = jax.ShapeDtypeStruct((2 * m, cases), F32)

time: 88.5 us -> 82.1 us (0.928)
  the two profiles are of different devices: /device:TPU:1 before, /device:TPU:23 now
where the time goes in v3:
time: 82.1 us; the launch traced here: 81.9 us
  Pallas kernels  78.2 us (95%)
  other arithmetic  3.11 us (4%)
    pallas_call x1, Pallas kernels, shards(): pl.pallas_call(functools.partial(kernel, nsec, nsub), out_shape=(out, out...  78.2 us
    sub x1, other arithmetic, shards(): residual = direction - turn * dual_load - second * image  3.11 us

profile of v3, /device:TPU:23, one launch (start us, length us, event | category | flops | bytes accessed | tf_op | source)
XLA Modules:
  0.0 81.9 jit_solution(5030895415278777590)
XLA Ops:
  0.6 0.0 copy-start
  0.6 78.2 %shard_map.68 = (f32[1024,256]{1,0:T(8,128)}, f32[1024,256]{1,0:T(8,128)}, f32[1,256]{1,0:T(1,128)}, f32[1,256]{1,0:T(1,128)}, f32[1,256]{1,0:T(1,128)}) custom-call(f32[1024,256]{1,0:T(8,128)} %bitcast.9, bf16[2048,2048]{1,0:T(8,128)(2,1)} %bitcast.15, s32[1,2048]{1,0:T(1,128)} %bitcast.16, s32[1,32]{1,0:T(1,128)} %bitcast.17, f32[512,512]{1,0:T(8,128)} %inverse_hbm.1), custom_call_target="tpu_custom_call" | custom-call | flops 17179869184 | bytes 8388608 | tf_op jit(solution)/shard_map/pallas_call | solution.py:625
  78.8 0.0 copy-done
  78.8 3.1 %multiply_subtract_fusion = (f32[1,1,2,512,256]{4,3,2,1,0:T(8,128)}, f32[1,1,2,512,256]{4,3,2,1,0:T(8,128)}) fusion(f32[1,1,2,512,256]{4,3,2,1,0:T(8,128)} %bitcast.11, f32[1,1,2,512,256]{4,3,2,1,0:T(8,128)} %bitcast.10, f32[1,1,2,512,256]{4,3,2,1,0:T(8,128)S(1)} %copy-done, f32[256]{0:T(256)} %bitcast.13, f32[256]{0:T(256)} %bitcast.14, f32[256]{0:T(256)} %bitcast.12), kind=kLoop, calls=%fused_computation | loop fusion | flops 1835008 | bytes 5245952 | tf_op jit(solution)/shard_map/sub | solution.py:648
Async XLA Ops:
  0.6 78.2 %copy-start = (f32[1,1,2,512,256]{4,3,2,1,0:T(8,128)S(1)}, f32[1,1,2,512,256]{4,3,2,1,0:T(8,128)}, u32[]{:S(2)}) copy-start(f32[1,1,2,512,256]{4,3,2,1,0:T(8,128)} %param.5) | copy-start | bytes 3145732
